TPU v7x, 32 devices: a whole 2x2x4 slice. The times are simulated.
32 devices in a mesh: streams: 2 (over y), span: 4 (over z), head: 2 (over x), seq: 2 (over core).
Axes of the slice: x: 2, y: 2, z: 4, core: 2. Of those that a mesh axis runs over, the one named last changes fastest.
Arguments:
- query_rows: bfloat16 [4096, 1280], P(('streams', 'span', 'seq'), 'head'), parts along dimension 0, may hold values from -100 to 100
- key_rows: bfloat16 [4096, 1280], P(('streams', 'span', 'seq'), 'head'), parts along dimension 0, may hold values from -5 to 5
- value_rows: bfloat16 [4096, 1280], P(('streams', 'span', 'seq'), 'head'), parts along dimension 0, may hold values from -6 to 6
- out_weight: bfloat16 [1280, 5120], P('head', 'seq'), may hold values from -0.59765625 to 0.59765625
- gate_table: float32 [4, 5120], P(None, 'head'), may hold values from 0.5 to 2
- step_index: int32 [8], P('streams'), parts along dimension 0, may hold values from 0 to 3
- block_mask: int32 [8, 4], P('streams'), parts along dimension 0, may hold values from 0 to 1, as said below
Outputs:
- gated_update: bfloat16 [4096, 5120], P(('streams', 'span', 'seq'), 'head'), parts along dimension 0
There are 2 independent parts, one for each index of `streams`. A program takes and returns all parts, laid end to end along the dimension named above; an argument that names none is the same for every part. Nothing has to cross between parts.
Inputs may be any that keep to these rules, and one draw needn't show every extreme that they name: block_mask[c, c] = 1 and block_mask[c, e] = 0 for e > c; entries below the diagonal are 0 or 1.
All inputs are finite; a program needn't handle non-finite values.
Results may differ from a plain program's by a relative error of at most 0.017.
Values may be sent and summed in bfloat16 or wider, within the bound.
A program may use at most 192 MiB of HBM per device.

v0:
```python
import math

import jax
import jax.numpy as jnp
from jax import lax
from jax.sharding import PartitionSpec as P

HD = 128


NEG_FLOOR = -1e30


def on_device(query_rows, key_rows, value_rows, out_weight, gate_table, step_index, block_mask):
    tok_rows = query_rows.shape[0]
    heads_here = query_rows.shape[1] // HD
    group_count = lax.axis_size("span")
    span_tok = tok_rows * lax.axis_size("seq")
    my_span = lax.axis_index("span")
    group_ids = jnp.arange(group_count, dtype=jnp.int32)
    mask_row = jnp.sum(jnp.where(group_ids[:, None] == my_span, block_mask, 0), axis=0)
    query_three = query_rows.reshape(tok_rows, heads_here, HD)
    score_scale = 1.0 / math.sqrt(HD)
    run_max = jnp.full((heads_here, tok_rows), NEG_FLOOR, jnp.float32)
    key_part = lax.all_gather(key_rows, ("span", "seq"), axis=0, tiled=True)
    value_part = lax.all_gather(value_rows, ("span", "seq"), axis=0, tiled=True)
    piece_rows = key_part.shape[0]
    key_group = jnp.arange(piece_rows, dtype=jnp.int32) // span_tok
    visible = (
        jnp.sum(jnp.where(key_group[:, None] == group_ids[None, :], mask_row[None, :], 0), axis=1)
        == 1
    )
    scores = (
        jnp.einsum(
            "thd,khd->htk",
            query_three,
            key_part.reshape(piece_rows, heads_here, HD),
            preferred_element_type=jnp.float32,
        )
        * score_scale
    )
    scores = jnp.where(visible[None, None, :], scores, NEG_FLOOR)
    new_max = jnp.maximum(run_max, jnp.max(scores, axis=2))
    probs = jnp.where(visible[None, None, :], jnp.exp(scores - new_max[:, :, None]), 0.0)
    run_total = jnp.sum(probs, axis=2)
    added = jnp.einsum(
        "htk,khd->htd",
        probs.astype(jnp.bfloat16),
        value_part.reshape(piece_rows, heads_here, HD),
        preferred_element_type=jnp.float32,
    )
    run_accum = added
    run_max, run_total, run_accum = (new_max, run_total, run_accum)
    summed = run_accum / run_total[:, :, None]
    attended = (
        jnp.transpose(summed, (1, 0, 2)).reshape(tok_rows, heads_here * HD).astype(jnp.bfloat16)
    )
    projected = jnp.dot(
        attended,
        lax.all_gather(out_weight, "seq", axis=1, tiled=True),
        preferred_element_type=jnp.float32,
    )
    shared = lax.psum_scatter(
        projected.astype(jnp.bfloat16), "head", scatter_dimension=1, tiled=True
    ).astype(jnp.float32)
    my_step = jnp.sum(jnp.where(group_ids == my_span, step_index, 0))
    step_ids = jnp.arange(gate_table.shape[0], dtype=jnp.int32)
    gate_row = jnp.sum(jnp.where((step_ids == my_step)[:, None], gate_table, 0.0), axis=0)
    return (gate_row[None, :] * shared).astype(jnp.bfloat16)


def solution(mesh):
    in_specs = (
        P(("streams", "span", "seq"), "head"),
        P(("streams", "span", "seq"), "head"),
        P(("streams", "span", "seq"), "head"),
        P("head", "seq"),
        P(None, "head"),
        P("streams"),
        P("streams", None),
    )
    out_specs = P(("streams", "span", "seq"), "head")
    return jax.shard_map(
        on_device, mesh=mesh, in_specs=in_specs, out_specs=out_specs, check_vma=False
    )
```

profile of v0, /device:TPU:9, one launch (start us, length us, event | category | flops | bytes accessed | tf_op | source)
XLA Modules:
  0.0 151.6 jit_solution(9862988004682840681)
XLA Ops:
  6.5 0.0 all-gather.6.cloned.1.call-start
  6.5 0.7 all-gather.6.cloned.1.call-update
  7.3 0.0 all-gather.4.cloned.1.call-start
  7.3 1.9 %copy.16 = bf16[256,640]{0,1:T(8,128)(2,1)} copy(bf16[256,640]{1,0:T(8,128)(2,1)} %param.8) | data formatting | bytes 655360 | tf_op args[1]
  9.2 0.0 all-gather.4.cloned.1.call-update
  9.2 0.0 all-gather.8.cloned.1.call-start
  9.2 0.7 all-gather.8.cloned.1.call-update
  9.9 0.0 reduce-scatter.2.cloned.1.call-start
  10.0 1.1 copy.15
  11.2 0.8 select_reduce_fusion.2
  11.9 0.1 select_reduce_fusion.1
  12.0 31.8 %all-gather.6.cloned.1.call-done = bf16[2048,640]{1,0:T(8,128)(2,1)} async-done(((bf16[256,640]{1,0:T(8,128)(2,1)}), bf16[2048,640]{1,0:T(8,128)(2,1)}) %all-gather.6.cloned.1.call-update) | async-done | bytes 2621456 | tf_op jit(solution)/shard_map/all_gather | solution.py:26
  43.8 3.0 %copy.19 = bf16[2048,640]{0,1:T(8,128)(2,1)S(1)} copy(bf16[2048,640]{1,0:T(8,128)(2,1)} %all-gather.6.cloned.1.call-done) | data formatting | bytes 5242880 | tf_op jit(solution)/shard_map/all_gather | solution.py:26
  46.8 33.1 %all-gather.4.cloned.1.call-done = bf16[2048,640]{0,1:T(8,128)(2,1)} async-done(((bf16[256,640]{0,1:T(8,128)(2,1)}), bf16[2048,640]{0,1:T(8,128)(2,1)}) %all-gather.4.cloned.1.call-update) | async-done | bytes 2621456 | tf_op jit(solution)/shard_map/all_gather | solution.py:25
  79.9 3.7 %fusion = (f32[5,256]{1,0:T(8,128)S(1)}, f32[5,256,2048]{2,1,0:T(8,128)S(1)}) fusion(pred[2048]{0:T(1024)(128)(4,1)S(1)} %broadcast_compare_fusion, bf16[256,5,128]{0,2,1:T(8,128)(2,1)S(1)} %bitcast.18, bf16[2048,5,128]{0,2,1:T(8,128)(2,1)} %bitcast.16), kind=kOutput, calls=%fused_computation.2 | convolution fusion | flops 678951680 | bytes 13442048 | tf_op jit(solution)/shard_map/thd,khd->htk/dot_general | solution.py:34
  83.6 2.6 %fusion.1 = f32[5,256]{1,0:T(8,128)S(1)} fusion(f32[5,256,2048]{2,1,0:T(8,128)S(1)} %get-tuple-element.6, f32[5,256]{1,0:T(8,128)S(1)} %broadcast_maximum_fusion, pred[2048]{0:T(1024)(128)(4,1)S(1)} %broadcast_compare_fusion), kind=kLoop, calls=%fused_computation.3 | loop fusion | flops 13105920 | bytes 10498048 | tf_op jit(solution)/shard_map/reduce_sum | solution.py:45
  86.1 3.3 %fusion.12 = bf16[256,5,128]{0,2,1:T(8,128)(2,1)S(1)} fusion(bf16[2048,5,128]{0,2,1:T(8,128)(2,1)S(1)} %bitcast.17, f32[5,256,2048]{2,1,0:T(8,128)S(1)} %get-tuple-element.6, f32[5,256]{1,0:T(8,128)S(1)} %broadcast_maximum_fusion, pred[2048]{0:T(1024)(128)(4,1)S(1)} %broadcast_compare_fusion, f32[256,5]{0,1:T(8,128)S(1)} %bitcast.20), kind=kOutput, calls=%fused_computation.11 | convolution fusion | flops 684523520 | bytes 13447168 | tf_op jit(solution)/shard_map/htk,khd->htd/dot_general | solution.py:46
  89.4 8.1 %all-gather.8.cloned.1.call-done = bf16[640,5120]{1,0:T(8,128)(2,1)} async-done(((bf16[640,2560]{1,0:T(8,128)(2,1)}), bf16[640,5120]{1,0:T(8,128)(2,1)}) %all-gather.8.cloned.1.call-update) | async-done | bytes 6553616 | tf_op jit(solution)/shard_map/all_gather | solution.py:60
  97.6 0.0 copy-start.1
  97.6 0.0 copy-start
  97.6 6.7 %convolution_convert_fusion = bf16[256,5120]{1,0:T(8,128)(2,1)} fusion(bf16[256,640]{0,1:T(8,128)(2,1)S(1)} %bitcast.19, bf16[640,5120]{1,0:T(8,128)(2,1)} %all-gather.8.cloned.1.call-done), kind=kOutput, calls=%fused_computation.5 | convolution fusion | flops 1679032320 | bytes 9502720 | tf_op jit(solution)/shard_map/dot_general | solution.py:58
  104.2 0.0 reduce-scatter.2.cloned.1.call-update
  104.3 0.0 copy-done.1
  104.3 0.6 select_reduce_fusion.3
  104.9 0.6 iota_compare_fusion.2
  105.6 0.0 copy-done
  105.6 0.1 select_reduce_fusion
  105.7 36.8 %reduce-scatter.2.cloned.1.call-done = bf16[256,2560]{1,0:T(8,128)(2,1)} async-done(((bf16[256,5120]{1,0:T(8,128)(2,1)}), bf16[256,2560]{1,0:T(8,128)(2,1)}) %reduce-scatter.2.cloned.1.call-update) | async-done | bytes 1310736 | tf_op jit(solution)/shard_map/reduce_scatter | solution.py:63
  142.4 2.6 %multiply_convert_fusion = bf16[256,2560]{1,0:T(8,128)(2,1)} fusion(bf16[256,2560]{1,0:T(8,128)(2,1)} %reduce-scatter.2.cloned.1.call-done, f32[2560]{0:T(1024)S(1)} %select_reduce_fusion), kind=kLoop, calls=%fused_computation.8 | loop fusion | flops 1966080 | bytes 2631680 | tf_op jit(solution)/shard_map/convert_element_type | solution.py:69
  (4 shorter events, 0.0 us)
Async XLA Ops:
  6.5 37.3 %all-gather.6.cloned.1.call-start = ((), (), s32[]{:S(2)}) async-start(), calls=%async_computation.2 | async-start | bytes 2949120 | tf_op jit(solution)/shard_map/all_gather | solution.py:26
  7.3 72.6 %all-gather.4.cloned.1.call-start = ((), (), s32[]{:S(2)}) async-start(), calls=%async_computation.1 | async-start | bytes 2949120 | tf_op jit(solution)/shard_map/all_gather | solution.py:25
  9.2 88.4 %all-gather.8.cloned.1.call-start = ((), (), s32[]{:S(2)}) async-start(), calls=%async_computation.3 | async-start | bytes 9830400 | tf_op jit(solution)/shard_map/all_gather | solution.py:60
  9.9 132.5 %reduce-scatter.2.cloned.1.call-start = ((), (), s32[]{:S(2)}) async-start(), calls=%async_computation.4 | async-start | bytes 3932160 | tf_op jit(solution)/shard_map/reduce_scatter | solution.py:63
  97.6 6.7 %copy-start.1 = (s32[4]{0:T(128)S(1)}, s32[4]{0:T(128)}, u32[]{:S(2)}) copy-start(s32[4]{0:T(128)} %param.12) | copy-start | bytes 52
  97.6 8.0 %copy-start = (f32[4,2560]{1,0:T(4,128)S(1)}, f32[4,2560]{1,0:T(4,128)}, u32[]{:S(2)}) copy-start(f32[4,2560]{1,0:T(4,128)} %param.11) | copy-start | bytes 122884
Sparse Core Ops, SparseCore 0:
  9.0 34.7 all-gather.5
  45.4 34.4 all-gather.3
  81.4 16.0 all-gather.7
  104.4 38.0 reduce-scatter.1
where the time goes:
time: 153 us; the launch traced here: 152 us
  waiting for transfers between devices  111 us (73%)
  matrix products  13.6 us (9%)
  between operations  13.2 us (9%)
  other arithmetic  7.42 us (5%)
  local copies, waits for them, and re-layouts  6.01 us (4%)
    reduce_scatter x1, waiting for transfers between devices, on_device(): lax.psum_scatter(projected.astype(jnp.bfloat16), 'head', scatter_dimensio...  36.8 us
    all_gather x1, waiting for transfers between devices, on_device(): key_part = lax.all_gather(key_rows, ('span', 'seq'), axis=0, tiled=True)  33.1 us
    all_gather x1, waiting for transfers between devices, on_device(): value_part = lax.all_gather(value_rows, ('span', 'seq'), axis=0, tiled=True)  31.8 us
    all_gather x1, waiting for transfers between devices, on_device(): lax.all_gather(out_weight, 'seq', axis=1, tiled=True)  8.12 us
    dot_general x1, matrix products, on_device(): jnp.dot(attended, lax.all_gather(out_weight, 'seq', axis=1, tiled=True),...  6.68 us
    dot_general x1, matrix products, on_device(): jnp.einsum('thd,khd->htk', query_three, key_part.reshape(piece_rows, head...  3.66 us
    dot_general x1, matrix products, on_device(): jnp.einsum('htk,khd->htd', probs.astype(jnp.bfloat16), value_part.reshape...  3.29 us
  transfers between devices with their start and end apart: 4, of which 4 were waited for; matrix products, arithmetic and copies ran while one was open for 12% of the time, Pallas kernels for 0%

commit v1 on v0

v1 whole, which is shorter than its diff:
```python
import functools
import math

import jax
import jax.numpy as jnp
from jax import lax
from jax.experimental import pallas as pl
from jax.experimental.pallas import tpu as pltpu
from jax.sharding import PartitionSpec as P

HD = 128
NEG_FLOOR = -1e30
MESH = pl.DeviceIdType.MESH
SCORE_SCALE = math.log2(math.e) / math.sqrt(HD)


def kernel(
    sizes,
    step_ref,
    mask_ref,
    q_ref,
    k_ref,
    v_ref,
    w_ref,
    gate_ref,
    out_ref,
    q_all,
    k_own,
    v_own,
    k_zero,
    v_zero,
    part_acc,
    part_stat,
    acc_out,
    stat_out,
    acc_in,
    stat_in,
    att,
    w_full,
    load_sem,
    sib_send,
    sib_recv,
    zero_send,
    zero_recv,
    fwd_send,
    fwd_recv,
    q_send,
    q_recv,
    acc_send,
    acc_recv,
    stat_send,
    stat_recv,
    x_send,
    x_recv,
    y_send,
    y_recv,
    d_send,
    d_recv,
    own_load,
    own_send,
    own_recv,
    att_send,
    att_recv,
):
    n_str, n_span, n_head, n_seq = sizes
    y = lax.axis_index("streams")
    z = lax.axis_index("span")
    x = lax.axis_index("head")
    s = lax.axis_index("seq")
    sib = 1 - s
    tok = q_ref.shape[0]
    heads = q_ref.shape[1] // HD
    w_rows = w_ref.shape[0]
    cols = out_ref.shape[1]
    y_rows = w_rows // n_str
    sub_rows = y_rows // n_seq
    piece = sub_rows // heads
    own_piece = w_rows // heads

    def remote(src, dst, ss, rs, **where):
        return pltpu.make_async_remote_copy(
            src_ref=src, dst_ref=dst, send_sem=ss, recv_sem=rs, device_id=where, device_id_type=MESH
        )

    def head_cols(h):
        return pl.ds(pl.multiple_of(h * HD, HD), HD)

    def each_head(body):
        lax.fori_loop(0, heads, lambda h, c: (body(h), c)[1], 0)

    def down(body, low):
        lax.fori_loop(0, n_span - low, lambda i, c: (body(n_span - 1 - i), c)[1], 0)

    tok_half = pl.ds(pl.multiple_of(s * tok, tok), tok)
    sib_half = pl.ds(pl.multiple_of(sib * tok, tok), tok)

    def load_q(h):
        return pltpu.make_async_copy(q_ref.at[:, head_cols(h)], q_all.at[z, h], load_sem.at[0, h])

    def load_k(h):
        return pltpu.make_async_copy(
            k_ref.at[:, head_cols(h)], k_own.at[h, tok_half], load_sem.at[1, h]
        )

    def load_v(h):
        return pltpu.make_async_copy(
            v_ref.at[:, head_cols(h)], v_own.at[h, tok_half], load_sem.at[2, h]
        )

    def sib_k(h, half):
        return remote(
            k_ref.at[:, head_cols(h)], k_own.at[h, half], sib_send.at[0, h], sib_recv.at[0, h], seq=sib
        )

    def sib_v(h, half):
        return remote(
            v_ref.at[:, head_cols(h)], v_own.at[h, half], sib_send.at[1, h], sib_recv.at[1, h], seq=sib
        )

    def zero_k(h):
        return remote(
            k_ref.at[:, head_cols(h)], k_zero.at[h, tok_half], zero_send.at[0, h], zero_recv.at[0, h],
            span=1,
        )

    def zero_v(h):
        return remote(
            v_ref.at[:, head_cols(h)], v_zero.at[h, tok_half], zero_send.at[1, h], zero_recv.at[1, h],
            span=1,
        )

    def fwd_k(h, half):
        return remote(
            k_zero.at[h, half], k_zero.at[h, half], fwd_send.at[0, h], fwd_recv.at[0, h], seq=sib
        )

    def fwd_v(h, half):
        return remote(
            v_zero.at[h, half], v_zero.at[h, half], fwd_send.at[1, h], fwd_recv.at[1, h], seq=sib
        )

    def own_q(h):
        return remote(
            q_ref.at[:, head_cols(h)], q_all.at[z, h], q_send.at[z, h], q_recv.at[z, h], span=z - 1
        )

    def pass_q(c, h):
        return remote(q_all.at[c, h], q_all.at[c, h], q_send.at[c, h], q_recv.at[c, h], span=z - 1)

    def pass_acc(c, h):
        return remote(
            acc_out.at[c, h], acc_in.at[c, h], acc_send.at[c, h], acc_recv.at[c, h], span=z + 1
        )

    def pass_stat(c, h):
        return remote(
            stat_out.at[c, h], stat_in.at[c, h], stat_send.at[c, h], stat_recv.at[c, h], span=z + 1
        )

    def w_at(src_x, part, sub, i):
        first = src_x * w_rows + part * y_rows + sub * sub_rows + i * piece
        return w_full.at[pl.ds(pl.multiple_of(first, piece), piece)]

    def block_core(dst_x):
        return (dst_x * n_seq) // n_head

    def block_cols(dst_x):
        first = lax.rem(dst_x, n_head // n_seq) * cols
        return pl.ds(pl.multiple_of(first, HD), cols)

    def x_piece(dst_x, sub, i):
        first = y * y_rows + sub * sub_rows + i * piece
        return remote(
            w_ref.at[pl.ds(pl.multiple_of(first, piece), piece), block_cols(dst_x)],
            w_at(x, y, sub, i),
            x_send.at[dst_x, sub, i],
            x_recv.at[x, i],
            head=dst_x,
            seq=sub,
        )

    def x_wait(src_x, i):
        ref = w_at(src_x, y, s, i)
        remote(ref, ref, x_send.at[src_x, 0, i], x_recv.at[src_x, i], head=src_x).wait_recv()

    def y_piece(src_x, dy, i):
        ref = w_at(src_x, y, s, i)
        return remote(
            ref, ref, y_send.at[src_x, dy, i], y_recv.at[src_x, dy, i], streams=lax.rem(y + dy, n_str)
        )

    def y_wait(src_x, dy, i):
        from_y = lax.rem(y - dy + n_str, n_str)
        ref = w_at(src_x, from_y, s, i)
        remote(
            ref, ref, y_send.at[src_x, dy, i], y_recv.at[src_x, dy, i], streams=from_y
        ).wait_recv()

    def d_piece(src_x, dy, i, sub):
        ref = w_at(src_x, lax.rem(y - dy + n_str, n_str), sub, i)
        return remote(ref, ref, d_send.at[src_x, dy, i], d_recv.at[src_x, dy, i], seq=sib)

    def own_rows(i):
        return pl.ds(pl.multiple_of(i * own_piece, own_piece), own_piece)

    def own_at(i):
        first = x * w_rows + i * own_piece
        return w_full.at[pl.ds(pl.multiple_of(first, own_piece), own_piece)]

    def own_copy(i):
        return pltpu.make_async_copy(w_ref.at[own_rows(i), block_cols(x)], own_at(i), own_load.at[i])

    def own_share(i):
        return remote(
            w_ref.at[own_rows(i), block_cols(x)], own_at(i), own_send.at[i], own_recv.at[i], seq=sib
        )

    def att_piece(dst_x, h):
        ref = att.at[x * heads + h]
        return remote(ref, ref, att_send.at[dst_x, h], att_recv.at[x, h], head=dst_x)

    def att_wait(src_x, h):
        ref = att.at[src_x * heads + h]
        remote(ref, ref, att_send.at[src_x, h], att_recv.at[src_x, h], head=src_x).wait_recv()

    others = [lax.rem(x + dx, n_head) for dx in range(1, n_head)]

    barrier = pltpu.get_barrier_semaphore()

    def greet(**where):
        pl.semaphore_signal(barrier, inc=1, device_id=where, device_id_type=MESH)

    greet(seq=sib)
    for other in others:
        for core in range(n_seq):
            greet(head=other, seq=core)
    for dy in range(1, n_str):
        greet(streams=lax.rem(y + dy, n_str))

    @pl.when(z > 0)
    def _():
        greet(span=z - 1)

    @pl.when(z < n_span - 1)
    def _():
        greet(span=z + 1)

    each_head(lambda h: (load_q(h).start(), load_k(h).start(), load_v(h).start()))
    beside = jnp.where(z > 0, 1, 0) + jnp.where(z < n_span - 1, 1, 0)
    pl.semaphore_wait(barrier, 1 + n_seq * (n_head - 1) + (n_str - 1) + beside)

    @pl.when(z >= 2)
    def _():
        own_q(0).start()

    @pl.when(z == 0)
    def _():
        each_head(lambda h: (zero_k(h).start(), zero_v(h).start()))

    each_head(lambda h: (sib_k(h, tok_half).start(), sib_v(h, tok_half).start()))
    for other in others:

        @pl.when(block_core(other) == s)
        def _(other=other):
            each_head(lambda i: [x_piece(other, sub, i).start() for sub in range(n_seq)])

    def block(q, k, v_t, flag):
        scores = (
            lax.dot_general(k, q, (((1,), (1,)), ((), ())), preferred_element_type=jnp.float32)
            * SCORE_SCALE
        )
        top = jnp.max(scores, axis=0, keepdims=True)
        probs = jnp.exp2(scores - top)
        total = jnp.sum(probs, axis=0, keepdims=True)
        acc = jnp.dot(v_t, probs.astype(jnp.bfloat16), preferred_element_type=jnp.float32)
        return jnp.where(flag == 1, top, NEG_FLOOR), total, acc

    def merge(a, b):
        top = jnp.maximum(a[0], b[0])
        wa, wb = jnp.exp2(a[0] - top), jnp.exp2(b[0] - top)
        return top, wa * a[1] + wb * b[1], wa * a[2] + wb * b[2]

    def get_part(c, h):
        return part_stat[c, h, 0:1], part_stat[c, h, 1:2], part_acc[c, h]

    def put_part(c, h, part):
        part_stat[c, h, 0:1] = part[0]
        part_stat[c, h, 1:2] = part[1]
        part_acc[c, h] = part[2]

    def emit(c, h, part):
        @pl.when(c > z)
        def _():
            stat_out[c, h, 0:1] = part[0]
            stat_out[c, h, 1:2] = part[1]
            acc_out[c, h] = part[2].astype(jnp.bfloat16)
            pass_acc(c, h).start()
            pass_stat(c, h).start()

        @pl.when(c == z)
        def _():
            att[x * heads + h] = (part[2] / part[1]).T.astype(jnp.bfloat16)
            for other in others:
                att_piece(other, h).start()

    def pass_on(h):
        def one(c):
            pass_q(c, h).wait_recv()

            @pl.when(z >= 2)
            def _():
                pass_q(c, h).start()

        down(one, z + 1)

        @pl.when((z >= 2) & (h + 1 < heads))
        def _():
            own_q(h + 1).start()

    @pl.when(z >= 2)
    def _():
        pass_on(0)

    def head_step(h):
        @pl.when((z >= 2) & (h + 1 < heads))
        def _():
            pass_on(h + 1)

        @pl.when(z == 1)
        def _():
            zero_k(h).wait_recv()
            fwd_k(h, tok_half).start()
            zero_v(h).wait_recv()
            fwd_v(h, tok_half).start()
            pass_on(h)

        @pl.when(block_core(x) == s)
        def _():
            own_copy(h).start()
            own_share(h).start()

        load_q(h).wait()
        load_k(h).wait()
        load_v(h).wait()
        sib_k(h, sib_half).wait_recv()
        sib_v(h, sib_half).wait_recv()

        k_here = k_own[h]
        v_here = v_own[h].T

        def own_block(c):
            put_part(c, h, block(q_all[c, h], k_here, v_here, mask_ref[c, z]))

        down(own_block, z)

        @pl.when(z == 1)
        def _():
            fwd_k(h, sib_half).wait_recv()
            fwd_v(h, sib_half).wait_recv()
            k_first = k_zero[h]
            v_first = v_zero[h].T

            def first_block(c):
                first = block(q_all[c, h], k_first, v_first, mask_ref[c, 0])
                emit(c, h, merge(get_part(c, h), first))

            down(first_block, z)

        @pl.when(z == 0)
        def _():
            emit(z, h, get_part(z, h))

        for other in others:
            x_wait(other, h)
            for dy in range(1, n_str):
                y_piece(other, dy, h).start()
            d_piece(other, 0, h, s).start()

            @pl.when(h > 0)
            def _(other=other):
                for dy in range(1, n_str):
                    y_wait(other, dy, h - 1)
                    d_piece(other, dy, h - 1, s).start()

    each_head(head_step)

    @pl.when(z >= 2)
    def _():
        def merge_step(h):
            def one(c):
                pass_acc(c, h).wait_recv()
                pass_stat(c, h).wait_recv()
                before = (
                    stat_in[c, h, 0:1],
                    stat_in[c, h, 1:2],
                    acc_in[c, h].astype(jnp.float32),
                )
                emit(c, h, merge(get_part(c, h), before))

            down(one, z)

        each_head(merge_step)

    for other in others:
        for dy in range(1, n_str):
            y_wait(other, dy, heads - 1)
            d_piece(other, dy, heads - 1, s).start()

    @pl.when(block_core(x) == s)
    def _():
        each_head(lambda i: own_copy(i).wait())

    @pl.when(block_core(x) != s)
    def _():
        each_head(lambda i: own_share(i).wait_recv())

    for other in others:

        def last_waits(i, other=other):
            for dy in range(n_str):
                d_piece(other, dy, i, sib).wait_recv()
            att_wait(other, i)

        each_head(last_waits)

    step = step_ref[z]
    tile = 256
    attended = jnp.concatenate([att[i] for i in range(n_head * heads)], axis=1)

    def project(t, carry):
        at = pl.ds(pl.multiple_of(t * tile, tile), tile)
        projected = jnp.dot(attended, w_full[:, at], preferred_element_type=jnp.float32)
        gate_row = jnp.zeros((1, tile), jnp.float32)
        for i in range(gate_ref.shape[0]):
            gate_row = jnp.where(step == i, gate_ref[i : i + 1, at], gate_row)
        out_ref[:, at] = (gate_row * projected).astype(jnp.bfloat16)
        return carry

    lax.fori_loop(0, cols // tile, project, 0)

    def sent(h):
        sib_k(h, tok_half).wait_send()
        sib_v(h, tok_half).wait_send()
        for other in others:
            att_piece(other, h).wait_send()
            for dy in range(1, n_str):
                y_piece(other, dy, h).wait_send()
            for dy in range(n_str):
                d_piece(other, dy, h, s).wait_send()

            @pl.when(block_core(other) == s)
            def _(other=other):
                for sub in range(n_seq):
                    x_piece(other, sub, h).wait_send()

        @pl.when(block_core(x) == s)
        def _():
            own_share(h).wait_send()

        @pl.when(z == 0)
        def _():
            zero_k(h).wait_send()
            zero_v(h).wait_send()

        @pl.when(z == 1)
        def _():
            fwd_k(h, tok_half).wait_send()
            fwd_v(h, tok_half).wait_send()

        @pl.when(z >= 2)
        def _():
            own_q(h).wait_send()
            down(lambda c: pass_q(c, h).wait_send(), z + 1)

        @pl.when(z >= 1)
        def _():
            down(lambda c: (pass_acc(c, h).wait_send(), pass_stat(c, h).wait_send()), z + 1)

    each_head(sent)


def solution(mesh):
    n_str, n_span = mesh.shape["streams"], mesh.shape["span"]
    n_head, n_seq = mesh.shape["head"], mesh.shape["seq"]
    sizes = (n_str, n_span, n_head, n_seq)

    def on_device(query_rows, key_rows, value_rows, out_weight, gate_table, step_index, block_mask):
        tok = query_rows.shape[0]
        heads = query_rows.shape[1] // HD
        cols = gate_table.shape[1]
        vmem, any_space = pltpu.VMEM, pl.ANY
        dma = pltpu.SemaphoreType.DMA
        low, wide = jnp.bfloat16, jnp.float32
        flops = 4 * heads * tok * tok * n_seq * n_span * HD + 2 * tok * n_head * heads * HD * cols
        return pl.pallas_call(
            functools.partial(kernel, sizes),
            out_shape=jax.ShapeDtypeStruct((tok, cols), low),
            in_specs=[
                pl.BlockSpec(memory_space=pltpu.SMEM),
                pl.BlockSpec(memory_space=pltpu.SMEM),
                pl.BlockSpec(memory_space=any_space),
                pl.BlockSpec(memory_space=any_space),
                pl.BlockSpec(memory_space=any_space),
                pl.BlockSpec(memory_space=any_space),
                pl.BlockSpec(memory_space=vmem),
            ],
            out_specs=pl.BlockSpec(memory_space=vmem),
            scratch_shapes=[
                vmem((n_span, heads, tok, HD), low),
                vmem((heads, n_seq * tok, HD), low),
                vmem((heads, n_seq * tok, HD), low),
                vmem((heads, n_seq * tok, HD), low),
                vmem((heads, n_seq * tok, HD), low),
                vmem((n_span, heads, HD, tok), wide),
                vmem((n_span, heads, 8, tok), wide),
                vmem((n_span, heads, HD, tok), low),
                vmem((n_span, heads, 8, tok), wide),
                vmem((n_span, heads, HD, tok), low),
                vmem((n_span, heads, 8, tok), wide),
                vmem((n_head * heads, tok, HD), low),
                vmem((n_head * heads * HD, cols), low),
                dma((3, heads)),
                dma((2, heads)),
                dma((2, heads)),
                dma((2, heads)),
                dma((2, heads)),
                dma((2, heads)),
                dma((2, heads)),
                dma((n_span, heads)),
                dma((n_span, heads)),
                dma((n_span, heads)),
                dma((n_span, heads)),
                dma((n_span, heads)),
                dma((n_span, heads)),
                dma((n_head, n_seq, heads)),
                dma((n_head, heads)),
                dma((n_head, n_str, heads)),
                dma((n_head, n_str, heads)),
                dma((n_head, n_str, heads)),
                dma((n_head, n_str, heads)),
                dma((heads,)),
                dma((heads,)),
                dma((heads,)),
                dma((n_head, heads)),
                dma((n_head, heads)),
            ],
            compiler_params=pltpu.CompilerParams(
                collective_id=0, has_side_effects=True, vmem_limit_bytes=56 * 1024 * 1024
            ),
            cost_estimate=pl.CostEstimate(
                flops=flops, bytes_accessed=6 * out_weight.size, transcendentals=0
            ),
        )(step_index, block_mask, query_rows, key_rows, value_rows, out_weight, gate_table)

    in_specs = (
        P(("streams", "span", "seq"), "head"),
        P(("streams", "span", "seq"), "head"),
        P(("streams", "span", "seq"), "head"),
        P("head", "seq"),
        P(None, "head"),
        P("streams"),
        P("streams", None),
    )
    out_specs = P(("streams", "span", "seq"), "head")
    return jax.shard_map(
        on_device, mesh=mesh, in_specs=in_specs, out_specs=out_specs, check_vma=False
    )
```

time: 153 us -> 51.5 us (0.34)
  the two profiles are of different devices: /device:TPU:9 before, /device:TPU:24 now
where the time goes in v1:
time: 51.5 us; the launch traced here: 51.3 us
  Pallas kernels  48.8 us (95%)
  local copies, waits for them, and re-layouts  2.46 us (5%)
    pallas_call x1, Pallas kernels, on_device(): pl.pallas_call(functools.partial(kernel, sizes), out_shape=jax.ShapeDtype...  48.8 us
    unnamed x1, local copies, waits for them, and re-layouts  2.46 us

profile of v1, /device:TPU:24, one launch (start us, length us, event | category | flops | bytes accessed | tf_op | source)
XLA Modules:
  0.0 51.3 jit_solution(11896952885602539742)
XLA Ops:
  0.0 48.8 %shard_map.73 = bf16[256,2560]{1,0:T(8,128)(2,1)} custom-call(s32[4]{0:T(128)} %step_ref.1, s32[4,4]{1,0:T(4,128)} %mask_ref.1, bf16[256,640]{1,0:T(8,128)(2,1)} %q_ref.1, bf16[256,640]{1,0:T(8,128)(2,1)} %k_ref.1, bf16[256,640]{1,0:T(8,128)(2,1)} %v_ref.1, bf16[640,2560]{1,0:T(8,128)(2,1)} %w_ref.1, f32[4,2560]{1,0:T(4,128)} %gate_ref.1), custom_call_target="tpu_custom_call" | custom-call | flops 3019898880 | bytes 9830400 | tf_op jit(solution)/shard_map/pallas_call | solution.py:495
  48.8 2.5 %copy.9 = bf16[256,2560]{1,0:T(8,128)(2,1)} copy(bf16[256,2560]{1,0:T(8,128)(2,1)} %shard_map.73) | data formatting | bytes 2621440

commit v2 on v1

--- a/solution.py
+++ b/solution.py
@@ -37,6 +37,7 @@
     stat_in,
     att,
     w_full,
+    out_half,
     load_sem,
     sib_send,
     sib_recv,
@@ -54,13 +55,15 @@
     x_recv,
     y_send,
     y_recv,
-    d_send,
-    d_recv,
     own_load,
     own_send,
     own_recv,
     att_send,
     att_recv,
+    pair_send,
+    pair_recv,
+    out_send,
+    out_recv,
 ):
     n_str, n_span, n_head, n_seq = sizes
     y = lax.axis_index("streams")
@@ -72,9 +75,11 @@
     heads = q_ref.shape[1] // HD
     w_rows = w_ref.shape[0]
     cols = out_ref.shape[1]
+    half = cols // n_seq
+    tile = 256 if half % 256 == 0 else 128
+    tiles = half // tile
     y_rows = w_rows // n_str
-    sub_rows = y_rows // n_seq
-    piece = sub_rows // heads
+    piece = y_rows // heads
     own_piece = w_rows // heads
 
     def remote(src, dst, ss, rs, **where):
@@ -157,49 +162,45 @@
             stat_out.at[c, h], stat_in.at[c, h], stat_send.at[c, h], stat_recv.at[c, h], span=z + 1
         )
 
-    def w_at(src_x, part, sub, i):
-        first = src_x * w_rows + part * y_rows + sub * sub_rows + i * piece
+    def w_at(src_x, part, i):
+        first = src_x * w_rows + part * y_rows + i * piece
         return w_full.at[pl.ds(pl.multiple_of(first, piece), piece)]
 
     def block_core(dst_x):
         return (dst_x * n_seq) // n_head
 
-    def block_cols(dst_x):
-        first = lax.rem(dst_x, n_head // n_seq) * cols
-        return pl.ds(pl.multiple_of(first, HD), cols)
-
-    def x_piece(dst_x, sub, i):
-        first = y * y_rows + sub * sub_rows + i * piece
-        return remote(
-            w_ref.at[pl.ds(pl.multiple_of(first, piece), piece), block_cols(dst_x)],
-            w_at(x, y, sub, i),
-            x_send.at[dst_x, sub, i],
+    def block_cols(dst_x, core):
+        first = lax.rem(dst_x, n_head // n_seq) * cols + core * half
+        return pl.ds(pl.multiple_of(first, HD), half)
+
+    def x_piece(dst_x, core, i):
+        first = y * y_rows + i * piece
+        return remote(
+            w_ref.at[pl.ds(pl.multiple_of(first, piece), piece), block_cols(dst_x, core)],
+            w_at(x, y, i),
+            x_send.at[dst_x, core, i],
             x_recv.at[x, i],
             head=dst_x,
-            seq=sub,
+            seq=core,
         )
 
     def x_wait(src_x, i):
-        ref = w_at(src_x, y, s, i)
+        ref = w_at(src_x, y, i)
         remote(ref, ref, x_send.at[src_x, 0, i], x_recv.at[src_x, i], head=src_x).wait_recv()
 
     def y_piece(src_x, dy, i):
-        ref = w_at(src_x, y, s, i)
+        ref = w_at(src_x, y, i)
         return remote(
             ref, ref, y_send.at[src_x, dy, i], y_recv.at[src_x, dy, i], streams=lax.rem(y + dy, n_str)
         )
 
     def y_wait(src_x, dy, i):
         from_y = lax.rem(y - dy + n_str, n_str)
-        ref = w_at(src_x, from_y, s, i)
+        ref = w_at(src_x, from_y, i)
         remote(
             ref, ref, y_send.at[src_x, dy, i], y_recv.at[src_x, dy, i], streams=from_y
         ).wait_recv()
 
-    def d_piece(src_x, dy, i, sub):
-        ref = w_at(src_x, lax.rem(y - dy + n_str, n_str), sub, i)
-        return remote(ref, ref, d_send.at[src_x, dy, i], d_recv.at[src_x, dy, i], seq=sib)
-
     def own_rows(i):
         return pl.ds(pl.multiple_of(i * own_piece, own_piece), own_piece)
 
@@ -208,20 +209,34 @@
         return w_full.at[pl.ds(pl.multiple_of(first, own_piece), own_piece)]
 
     def own_copy(i):
-        return pltpu.make_async_copy(w_ref.at[own_rows(i), block_cols(x)], own_at(i), own_load.at[i])
+        return pltpu.make_async_copy(
+            w_ref.at[own_rows(i), block_cols(x, s)], own_at(i), own_load.at[i]
+        )
 
     def own_share(i):
         return remote(
-            w_ref.at[own_rows(i), block_cols(x)], own_at(i), own_send.at[i], own_recv.at[i], seq=sib
+            w_ref.at[own_rows(i), block_cols(x, sib)], own_at(i), own_send.at[i], own_recv.at[i], seq=sib
         )
 
     def att_piece(dst_x, h):
-        ref = att.at[x * heads + h]
+        ref = att.at[x * heads + h, tok_half]
         return remote(ref, ref, att_send.at[dst_x, h], att_recv.at[x, h], head=dst_x)
 
     def att_wait(src_x, h):
-        ref = att.at[src_x * heads + h]
+        ref = att.at[src_x * heads + h, tok_half]
         remote(ref, ref, att_send.at[src_x, h], att_recv.at[src_x, h], head=src_x).wait_recv()
+
+    def att_pair(src_x, h, rows):
+        ref = att.at[src_x * heads + h, rows]
+        return remote(ref, ref, pair_send.at[src_x, h], pair_recv.at[src_x, h], seq=sib)
+
+    def out_cols(core, t):
+        return pl.ds(pl.multiple_of(core * half + t * tile, tile), tile)
+
+    def out_piece(core, t):
+        return remote(
+            out_half.at[t], out_ref.at[:, out_cols(core, t)], out_send.at[t], out_recv.at[t], seq=sib
+        )
 
     others = [lax.rem(x + dx, n_head) for dx in range(1, n_head)]
 
@@ -299,9 +314,10 @@
 
         @pl.when(c == z)
         def _():
-            att[x * heads + h] = (part[2] / part[1]).T.astype(jnp.bfloat16)
+            att[x * heads + h, tok_half] = (part[2] / part[1]).T.astype(jnp.bfloat16)
             for other in others:
                 att_piece(other, h).start()
+            att_pair(x, h, tok_half).start()
 
     def pass_on(h):
         def one(c):
@@ -320,6 +336,12 @@
     @pl.when(z >= 2)
     def _():
         pass_on(0)
+
+    def pass_w(i):
+        for other in others:
+            x_wait(other, i)
+            for dy in range(1, n_str):
+                y_piece(other, dy, i).start()
 
     def head_step(h):
         @pl.when((z >= 2) & (h + 1 < heads))
@@ -370,19 +392,23 @@
         def _():
             emit(z, h, get_part(z, h))
 
-        for other in others:
-            x_wait(other, h)
-            for dy in range(1, n_str):
-                y_piece(other, dy, h).start()
-            d_piece(other, 0, h, s).start()
-
-            @pl.when(h > 0)
-            def _(other=other):
-                for dy in range(1, n_str):
-                    y_wait(other, dy, h - 1)
-                    d_piece(other, dy, h - 1, s).start()
+        @pl.when(z == 0)
+        def _():
+            pass_w(h)
+
+        @pl.when((z == 1) & (h > 0))
+        def _():
+            pass_w(h - 1)
+
+        @pl.when((z >= 2) & ((h == 2) | (h == 4)))
+        def _():
+            pass_w(h // 2 - 1)
 
     each_head(head_step)
+
+    @pl.when(z == 1)
+    def _():
+        pass_w(heads - 1)
 
     @pl.when(z >= 2)
     def _():
@@ -399,12 +425,19 @@
 
             down(one, z)
 
+            @pl.when(h + 2 < heads)
+            def _():
+                pass_w(h + 2)
+
         each_head(merge_step)
 
     for other in others:
-        for dy in range(1, n_str):
-            y_wait(other, dy, heads - 1)
-            d_piece(other, dy, heads - 1, s).start()
+
+        def pass_att(h, other=other):
+            att_wait(other, h)
+            att_pair(other, h, tok_half).start()
+
+        each_head(pass_att)
 
     @pl.when(block_core(x) == s)
     def _():
@@ -414,39 +447,53 @@
     def _():
         each_head(lambda i: own_share(i).wait_recv())
 
-    for other in others:
-
-        def last_waits(i, other=other):
-            for dy in range(n_str):
-                d_piece(other, dy, i, sib).wait_recv()
-            att_wait(other, i)
-
-        each_head(last_waits)
+    def last_waits(h):
+        for other in others:
+            for dy in range(1, n_str):
+                y_wait(other, dy, h)
+            att_pair(other, h, sib_half).wait_recv()
+        att_pair(x, h, sib_half).wait_recv()
+
+    each_head(last_waits)
 
     step = step_ref[z]
-    tile = 256
-    attended = jnp.concatenate([att[i] for i in range(n_head * heads)], axis=1)
+
+    def gathered(rows):
+        return jnp.concatenate([att[i, rows] for i in range(n_head * heads)], axis=1)
+
+    attended = jnp.concatenate([gathered(sib_half), gathered(tok_half)], axis=0)
 
     def project(t, carry):
         at = pl.ds(pl.multiple_of(t * tile, tile), tile)
         projected = jnp.dot(attended, w_full[:, at], preferred_element_type=jnp.float32)
+        here = out_cols(s, t)
         gate_row = jnp.zeros((1, tile), jnp.float32)
         for i in range(gate_ref.shape[0]):
-            gate_row = jnp.where(step == i, gate_ref[i : i + 1, at], gate_row)
-        out_ref[:, at] = (gate_row * projected).astype(jnp.bfloat16)
+            gate_row = jnp.where(step == i, gate_ref[i : i + 1, here], gate_row)
+        gated = (gate_row * projected).astype(jnp.bfloat16)
+        out_half[t] = gated[:tok]
+        out_piece(s, t).start()
+        out_ref[:, here] = gated[tok:]
         return carry
 
-    lax.fori_loop(0, cols // tile, project, 0)
+    lax.fori_loop(0, tiles, project, 0)
+
+    def out_wait(t, carry):
+        out_piece(sib, t).wait_recv()
+        out_piece(s, t).wait_send()
+        return carry
+
+    lax.fori_loop(0, tiles, out_wait, 0)
 
     def sent(h):
         sib_k(h, tok_half).wait_send()
         sib_v(h, tok_half).wait_send()
+        att_pair(x, h, tok_half).wait_send()
         for other in others:
             att_piece(other, h).wait_send()
             for dy in range(1, n_str):
                 y_piece(other, dy, h).wait_send()
-            for dy in range(n_str):
-                d_piece(other, dy, h, s).wait_send()
+            att_pair(other, h, tok_half).wait_send()
 
             @pl.when(block_core(other) == s)
             def _(other=other):
@@ -488,6 +535,9 @@
         tok = query_rows.shape[0]
         heads = query_rows.shape[1] // HD
         cols = gate_table.shape[1]
+        half = cols // n_seq
+        tile = 256 if half % 256 == 0 else 128
+        tiles = half // tile
         vmem, any_space = pltpu.VMEM, pl.ANY
         dma = pltpu.SemaphoreType.DMA
         low, wide = jnp.bfloat16, jnp.float32
@@ -517,8 +567,9 @@
                 vmem((n_span, heads, 8, tok), wide),
                 vmem((n_span, heads, HD, tok), low),
                 vmem((n_span, heads, 8, tok), wide),
-                vmem((n_head * heads, tok, HD), low),
-                vmem((n_head * heads * HD, cols), low),
+                vmem((n_head * heads, n_seq * tok, HD), low),
+                vmem((n_head * heads * HD, half), low),
+                vmem((tiles, tok, tile), low),
                 dma((3, heads)),
                 dma((2, heads)),
                 dma((2, heads)),
@@ -536,13 +587,15 @@
                 dma((n_head, heads)),
                 dma((n_head, n_str, heads)),
                 dma((n_head, n_str, heads)),
-                dma((n_head, n_str, heads)),
-                dma((n_head, n_str, heads)),
                 dma((heads,)),
                 dma((heads,)),
                 dma((heads,)),
                 dma((n_head, heads)),
                 dma((n_head, heads)),
+                dma((n_head, heads)),
+                dma((n_head, heads)),
+                dma((tiles,)),
+                dma((tiles,)),
             ],
             compiler_params=pltpu.CompilerParams(
                 collective_id=0, has_side_effects=True, vmem_limit_bytes=56 * 1024 * 1024

time: 51.5 us -> 50.7 us (0.984)
  the two profiles are of different devices: /device:TPU:24 before, /device:TPU:9 now
where the time goes in v2:
time: 50.7 us; the launch traced here: 49.9 us
  Pallas kernels  47.4 us (93%)
  local copies, waits for them, and re-layouts  2.46 us (5%)
    pallas_call x1, Pallas kernels, on_device(): pl.pallas_call(functools.partial(kernel, sizes), out_shape=jax.ShapeDtype...  47.4 us
    unnamed x1, local copies, waits for them, and re-layouts  2.46 us

profile of v2, /device:TPU:9, one launch (start us, length us, event | category | flops | bytes accessed | tf_op | source)
XLA Modules:
  0.0 49.9 jit_solution(12927889073805352956)
XLA Ops:
  0.0 47.4 %shard_map.73 = bf16[256,2560]{1,0:T(8,128)(2,1)} custom-call(s32[4]{0:T(128)} %step_ref.1, s32[4,4]{1,0:T(4,128)} %mask_ref.1, bf16[256,640]{1,0:T(8,128)(2,1)} %q_ref.1, bf16[256,640]{1,0:T(8,128)(2,1)} %k_ref.1, bf16[256,640]{1,0:T(8,128)(2,1)} %v_ref.1, bf16[640,2560]{1,0:T(8,128)(2,1)} %w_ref.1, f32[4,2560]{1,0:T(4,128)} %gate_ref.1), custom_call_target="tpu_custom_call" | custom-call | flops 3019898880 | bytes 9830400 | tf_op jit(solution)/shard_map/pallas_call | solution.py:545
  47.4 2.5 %copy.9 = bf16[256,2560]{1,0:T(8,128)(2,1)} copy(bf16[256,2560]{1,0:T(8,128)(2,1)} %shard_map.73) | data formatting | bytes 2621440

commit v3 on v2

--- a/solution.py
+++ b/solution.py
@@ -279,16 +279,24 @@
         def _(other=other):
             each_head(lambda i: [x_piece(other, sub, i).start() for sub in range(n_seq)])
 
-    def block(q, k, v_t, flag):
-        scores = (
+    def block(q, keys, v_t, flags):
+        scores = [
             lax.dot_general(k, q, (((1,), (1,)), ((), ())), preferred_element_type=jnp.float32)
             * SCORE_SCALE
-        )
-        top = jnp.max(scores, axis=0, keepdims=True)
-        probs = jnp.exp2(scores - top)
-        total = jnp.sum(probs, axis=0, keepdims=True)
-        acc = jnp.dot(v_t, probs.astype(jnp.bfloat16), preferred_element_type=jnp.float32)
-        return jnp.where(flag == 1, top, NEG_FLOOR), total, acc
+            for k in keys
+        ]
+        tops = [
+            jnp.where(flag == 1, jnp.max(each, axis=0, keepdims=True), NEG_FLOOR)
+            for each, flag in zip(scores, flags)
+        ]
+        top = functools.reduce(jnp.maximum, tops)
+        probs = [
+            jnp.exp2(each - jnp.where(flag == 1, top, -NEG_FLOOR))
+            for each, flag in zip(scores, flags)
+        ]
+        total = sum(jnp.sum(each, axis=0, keepdims=True) for each in probs)
+        low = jnp.concatenate([each.astype(jnp.bfloat16) for each in probs], axis=0)
+        return top, total, jnp.dot(v_t, low, preferred_element_type=jnp.float32)
 
     def merge(a, b):
         top = jnp.maximum(a[0], b[0])
@@ -370,23 +378,32 @@
         k_here = k_own[h]
         v_here = v_own[h].T
 
-        def own_block(c):
-            put_part(c, h, block(q_all[c, h], k_here, v_here, mask_ref[c, z]))
-
-        down(own_block, z)
+        @pl.when(z != 1)
+        def _():
+            def own_block(c):
+                put_part(c, h, block(q_all[c, h], [k_here], v_here, [mask_ref[c, z]]))
+
+            down(own_block, z)
 
         @pl.when(z == 1)
         def _():
             fwd_k(h, sib_half).wait_recv()
             fwd_v(h, sib_half).wait_recv()
-            k_first = k_zero[h]
-            v_first = v_zero[h].T
-
-            def first_block(c):
-                first = block(q_all[c, h], k_first, v_first, mask_ref[c, 0])
-                emit(c, h, merge(get_part(c, h), first))
-
-            down(first_block, z)
+            keys = [k_here, k_zero[h]]
+            both = jnp.concatenate([v_here, v_zero[h].T], axis=1)
+            group = 3 if (n_span - 1) % 3 == 0 else 1
+
+            def first_blocks(i, carry):
+                spans = [n_span - 1 - i * group - j for j in range(group)]
+                parts = [
+                    block(q_all[c, h], keys, both, [mask_ref[c, 1], mask_ref[c, 0]]) for c in spans
+                ]
+                for c, part in zip(spans, parts):
+                    put_part(c, h, part)
+                return carry
+
+            lax.fori_loop(0, (n_span - 1) // group, first_blocks, 0)
+            down(lambda c: emit(c, h, get_part(c, h)), 1)
 
         @pl.when(z == 0)
         def _():
@@ -396,9 +413,9 @@
         def _():
             pass_w(h)
 
-        @pl.when((z == 1) & (h > 0))
-        def _():
-            pass_w(h - 1)
+        @pl.when((z == 1) & (h > 1))
+        def _():
+            pass_w(h - 2)
 
         @pl.when((z >= 2) & ((h == 2) | (h == 4)))
         def _():
@@ -408,6 +425,7 @@
 
     @pl.when(z == 1)
     def _():
+        pass_w(heads - 2)
         pass_w(heads - 1)
 
     @pl.when(z >= 2)

time: 50.7 us -> 51.2 us (level); the launches traced: 49.9 us -> 51 us
  Pallas kernels: 47.4 us -> 48.5 us
    pallas_call x1, Pallas kernels: 47.4 us -> 48.5 us  [on_device(): pl.pallas_call(functools.partial(kernel, sizes), out_shape=jax.ShapeDtype...]
where the time goes in v3:
time: 51.2 us; the launch traced here: 51 us
  Pallas kernels  48.5 us (95%)
  local copies, waits for them, and re-layouts  2.46 us (5%)
    pallas_call x1, Pallas kernels, on_device(): pl.pallas_call(functools.partial(kernel, sizes), out_shape=jax.ShapeDtype...  48.5 us
    unnamed x1, local copies, waits for them, and re-layouts  2.46 us

profile of v3, /device:TPU:9, one launch (start us, length us, event | category | flops | bytes accessed | tf_op | source)
XLA Modules:
  0.0 51.0 jit_solution(12371878720217468630)
XLA Ops:
  0.0 48.5 %shard_map.73 = bf16[256,2560]{1,0:T(8,128)(2,1)} custom-call(s32[4]{0:T(128)} %step_ref.1, s32[4,4]{1,0:T(4,128)} %mask_ref.1, bf16[256,640]{1,0:T(8,128)(2,1)} %q_ref.1, bf16[256,640]{1,0:T(8,128)(2,1)} %k_ref.1, bf16[256,640]{1,0:T(8,128)(2,1)} %v_ref.1, bf16[640,2560]{1,0:T(8,128)(2,1)} %w_ref.1, f32[4,2560]{1,0:T(4,128)} %gate_ref.1), custom_call_target="tpu_custom_call" | custom-call | flops 3019898880 | bytes 9830400 | tf_op jit(solution)/shard_map/pallas_call | solution.py:563
  48.5 2.5 %copy.9 = bf16[256,2560]{1,0:T(8,128)(2,1)} copy(bf16[256,2560]{1,0:T(8,128)(2,1)} %shard_map.73) | data formatting | bytes 2621440

commit v4 on v3

--- a/solution.py
+++ b/solution.py
@@ -38,6 +38,9 @@
     att,
     w_full,
     out_half,
+    w_relay,
+    relay_send,
+    relay_recv,
     load_sem,
     sib_send,
     sib_recv,
@@ -114,24 +117,22 @@
 
     def sib_k(h, half):
         return remote(
-            k_ref.at[:, head_cols(h)], k_own.at[h, half], sib_send.at[0, h], sib_recv.at[0, h], seq=sib
+            k_own.at[h, half], k_own.at[h, half], sib_send.at[0, h], sib_recv.at[0, h], seq=sib
         )
 
     def sib_v(h, half):
         return remote(
-            v_ref.at[:, head_cols(h)], v_own.at[h, half], sib_send.at[1, h], sib_recv.at[1, h], seq=sib
+            v_own.at[h, half], v_own.at[h, half], sib_send.at[1, h], sib_recv.at[1, h], seq=sib
         )
 
     def zero_k(h):
         return remote(
-            k_ref.at[:, head_cols(h)], k_zero.at[h, tok_half], zero_send.at[0, h], zero_recv.at[0, h],
-            span=1,
+            k_own.at[h, tok_half], k_zero.at[h, tok_half], zero_send.at[0, h], zero_recv.at[0, h], span=1
         )
 
     def zero_v(h):
         return remote(
-            v_ref.at[:, head_cols(h)], v_zero.at[h, tok_half], zero_send.at[1, h], zero_recv.at[1, h],
-            span=1,
+            v_own.at[h, tok_half], v_zero.at[h, tok_half], zero_send.at[1, h], zero_recv.at[1, h], span=1
         )
 
     def fwd_k(h, half):
@@ -142,11 +143,6 @@
     def fwd_v(h, half):
         return remote(
             v_zero.at[h, half], v_zero.at[h, half], fwd_send.at[1, h], fwd_recv.at[1, h], seq=sib
-        )
-
-    def own_q(h):
-        return remote(
-            q_ref.at[:, head_cols(h)], q_all.at[z, h], q_send.at[z, h], q_recv.at[z, h], span=z - 1
         )
 
     def pass_q(c, h):
@@ -173,20 +169,38 @@
         first = lax.rem(dst_x, n_head // n_seq) * cols + core * half
         return pl.ds(pl.multiple_of(first, HD), half)
 
-    def x_piece(dst_x, core, i):
+    def x_piece(dst_x, i):
         first = y * y_rows + i * piece
         return remote(
-            w_ref.at[pl.ds(pl.multiple_of(first, piece), piece), block_cols(dst_x, core)],
+            w_ref.at[pl.ds(pl.multiple_of(first, piece), piece), block_cols(dst_x, s)],
             w_at(x, y, i),
-            x_send.at[dst_x, core, i],
+            x_send.at[dst_x, i],
             x_recv.at[x, i],
             head=dst_x,
-            seq=core,
+        )
+
+    def relay(dst_x, i):
+        first = y * y_rows + i * piece
+        return remote(
+            w_ref.at[pl.ds(pl.multiple_of(first, piece), piece), block_cols(dst_x, sib)],
+            w_relay.at[dst_x, i],
+            relay_send.at[dst_x, i],
+            relay_recv.at[dst_x, i],
+            seq=sib,
+        )
+
+    def x_relayed(dst_x, i):
+        return remote(
+            w_relay.at[dst_x, i],
+            w_at(x, y, i),
+            x_send.at[dst_x, i],
+            x_recv.at[x, i],
+            head=dst_x,
         )
 
     def x_wait(src_x, i):
         ref = w_at(src_x, y, i)
-        remote(ref, ref, x_send.at[src_x, 0, i], x_recv.at[src_x, i], head=src_x).wait_recv()
+        remote(ref, ref, x_send.at[src_x, i], x_recv.at[src_x, i], head=src_x).wait_recv()
 
     def y_piece(src_x, dy, i):
         ref = w_at(src_x, y, i)
@@ -264,9 +278,11 @@
     beside = jnp.where(z > 0, 1, 0) + jnp.where(z < n_span - 1, 1, 0)
     pl.semaphore_wait(barrier, 1 + n_seq * (n_head - 1) + (n_str - 1) + beside)
 
+    each_head(lambda h: (load_q(h).wait(), load_k(h).wait(), load_v(h).wait()))
+
     @pl.when(z >= 2)
     def _():
-        own_q(0).start()
+        pass_q(z, 0).start()
 
     @pl.when(z == 0)
     def _():
@@ -277,7 +293,7 @@
 
         @pl.when(block_core(other) == s)
         def _(other=other):
-            each_head(lambda i: [x_piece(other, sub, i).start() for sub in range(n_seq)])
+            each_head(lambda i: (relay(other, i).start(), x_piece(other, i).start()))
 
     def block(q, keys, v_t, flags):
         scores = [
@@ -339,7 +355,7 @@
 
         @pl.when((z >= 2) & (h + 1 < heads))
         def _():
-            own_q(h + 1).start()
+            pass_q(z, h + 1).start()
 
     @pl.when(z >= 2)
     def _():
@@ -351,6 +367,12 @@
             for dy in range(1, n_str):
                 y_piece(other, dy, i).start()
 
+    for other in others:
+
+        @pl.when(block_core(other) != s)
+        def _(other=other):
+            each_head(lambda i: (relay(other, i).wait_recv(), x_relayed(other, i).start()))
+
     def head_step(h):
         @pl.when((z >= 2) & (h + 1 < heads))
         def _():
@@ -369,9 +391,6 @@
             own_copy(h).start()
             own_share(h).start()
 
-        load_q(h).wait()
-        load_k(h).wait()
-        load_v(h).wait()
         sib_k(h, sib_half).wait_recv()
         sib_v(h, sib_half).wait_recv()
 
@@ -413,9 +432,9 @@
         def _():
             pass_w(h)
 
-        @pl.when((z == 1) & (h > 1))
-        def _():
-            pass_w(h - 2)
+        @pl.when((z == 1) & (h > 0))
+        def _():
+            pass_w(h - 1)
 
         @pl.when((z >= 2) & ((h == 2) | (h == 4)))
         def _():
@@ -425,7 +444,6 @@
 
     @pl.when(z == 1)
     def _():
-        pass_w(heads - 2)
         pass_w(heads - 1)
 
     @pl.when(z >= 2)
@@ -513,10 +531,11 @@
                 y_piece(other, dy, h).wait_send()
             att_pair(other, h, tok_half).wait_send()
 
+            x_piece(other, h).wait_send()
+
             @pl.when(block_core(other) == s)
             def _(other=other):
-                for sub in range(n_seq):
-                    x_piece(other, sub, h).wait_send()
+                relay(other, h).wait_send()
 
         @pl.when(block_core(x) == s)
         def _():
@@ -534,8 +553,7 @@
 
         @pl.when(z >= 2)
         def _():
-            own_q(h).wait_send()
-            down(lambda c: pass_q(c, h).wait_send(), z + 1)
+            down(lambda c: pass_q(c, h).wait_send(), z)
 
         @pl.when(z >= 1)
         def _():
@@ -556,6 +574,7 @@
         half = cols // n_seq
         tile = 256 if half % 256 == 0 else 128
         tiles = half // tile
+        piece = out_weight.shape[0] // n_str // heads
         vmem, any_space = pltpu.VMEM, pl.ANY
         dma = pltpu.SemaphoreType.DMA
         low, wide = jnp.bfloat16, jnp.float32
@@ -588,6 +607,9 @@
                 vmem((n_head * heads, n_seq * tok, HD), low),
                 vmem((n_head * heads * HD, half), low),
                 vmem((tiles, tok, tile), low),
+                vmem((n_head, heads, piece, half), low),
+                dma((n_head, heads)),
+                dma((n_head, heads)),
                 dma((3, heads)),
                 dma((2, heads)),
                 dma((2, heads)),
@@ -601,7 +623,7 @@
                 dma((n_span, heads)),
                 dma((n_span, heads)),
                 dma((n_span, heads)),
-                dma((n_head, n_seq, heads)),
+                dma((n_head, heads)),
                 dma((n_head, heads)),
                 dma((n_head, n_str, heads)),
                 dma((n_head, n_str, heads)),

time: 51.2 us -> 48.2 us (0.941)
  Pallas kernels: 48.5 us -> 45.5 us
    pallas_call x1, Pallas kernels: 48.5 us -> 45.5 us  [on_device(): pl.pallas_call(functools.partial(kernel, sizes), out_shape=jax.ShapeDtype...]
where the time goes in v4:
time: 48.2 us; the launch traced here: 47.9 us
  Pallas kernels  45.5 us (94%)
  local copies, waits for them, and re-layouts  2.46 us (5%)
    pallas_call x1, Pallas kernels, on_device(): pl.pallas_call(functools.partial(kernel, sizes), out_shape=jax.ShapeDtype...  45.5 us
    unnamed x1, local copies, waits for them, and re-layouts  2.46 us

profile of v4, /device:TPU:9, one launch (start us, length us, event | category | flops | bytes accessed | tf_op | source)
XLA Modules:
  0.0 47.9 jit_solution(525235136701804379)
XLA Ops:
  0.0 45.5 %shard_map.73 = bf16[256,2560]{1,0:T(8,128)(2,1)} custom-call(s32[4]{0:T(128)} %step_ref.1, s32[4,4]{1,0:T(4,128)} %mask_ref.1, bf16[256,640]{1,0:T(8,128)(2,1)} %q_ref.1, bf16[256,640]{1,0:T(8,128)(2,1)} %k_ref.1, bf16[256,640]{1,0:T(8,128)(2,1)} %v_ref.1, bf16[640,2560]{1,0:T(8,128)(2,1)} %w_ref.1, f32[4,2560]{1,0:T(4,128)} %gate_ref.1), custom_call_target="tpu_custom_call" | custom-call | flops 3019898880 | bytes 9830400 | tf_op jit(solution)/shard_map/pallas_call | solution.py:582
  45.5 2.5 %copy.9 = bf16[256,2560]{1,0:T(8,128)(2,1)} copy(bf16[256,2560]{1,0:T(8,128)(2,1)} %shard_map.73) | data formatting | bytes 2621440

commit v5 on v4

--- a/solution.py
+++ b/solution.py
@@ -39,6 +39,8 @@
     w_full,
     out_half,
     w_relay,
+    v_turned,
+    projected,
     relay_send,
     relay_recv,
     load_sem,
@@ -343,6 +345,11 @@
                 att_piece(other, h).start()
             att_pair(x, h, tok_half).start()
 
+    def pass_att(h):
+        for other in others:
+            att_wait(other, h)
+            att_pair(other, h, tok_half).start()
+
     def pass_on(h):
         def one(c):
             pass_q(c, h).wait_recv()
@@ -373,6 +380,19 @@
         def _(other=other):
             each_head(lambda i: (relay(other, i).wait_recv(), x_relayed(other, i).start()))
 
+    def share_zero(h):
+        zero_k(h).wait_recv()
+        fwd_k(h, tok_half).start()
+        zero_v(h).wait_recv()
+        fwd_v(h, tok_half).start()
+
+    @pl.when(z == 1)
+    def _():
+        share_zero(0)
+
+    def zero_block(c, h, v_t):
+        return block(q_all[c, h], [k_own[h], k_zero[h]], v_t, [mask_ref[c, 1], mask_ref[c, 0]])
+
     def head_step(h):
         @pl.when((z >= 2) & (h + 1 < heads))
         def _():
@@ -380,10 +400,6 @@
 
         @pl.when(z == 1)
         def _():
-            zero_k(h).wait_recv()
-            fwd_k(h, tok_half).start()
-            zero_v(h).wait_recv()
-            fwd_v(h, tok_half).start()
             pass_on(h)
 
         @pl.when(block_core(x) == s)
@@ -408,21 +424,17 @@
         def _():
             fwd_k(h, sib_half).wait_recv()
             fwd_v(h, sib_half).wait_recv()
-            keys = [k_here, k_zero[h]]
             both = jnp.concatenate([v_here, v_zero[h].T], axis=1)
-            group = 3 if (n_span - 1) % 3 == 0 else 1
-
-            def first_blocks(i, carry):
-                spans = [n_span - 1 - i * group - j for j in range(group)]
-                parts = [
-                    block(q_all[c, h], keys, both, [mask_ref[c, 1], mask_ref[c, 0]]) for c in spans
-                ]
-                for c, part in zip(spans, parts):
-                    put_part(c, h, part)
-                return carry
-
-            lax.fori_loop(0, (n_span - 1) // group, first_blocks, 0)
-            down(lambda c: emit(c, h, get_part(c, h)), 1)
+            v_turned[h] = both
+
+            def later(c):
+                emit(c, h, zero_block(c, h, both))
+
+                @pl.when((c == n_span - 1) & (h + 1 < heads))
+                def _():
+                    share_zero(h + 1)
+
+            down(later, 2)
 
         @pl.when(z == 0)
         def _():
@@ -444,7 +456,14 @@
 
     @pl.when(z == 1)
     def _():
-        pass_w(heads - 1)
+        def own_step(h):
+            emit(1, h, zero_block(1, h, v_turned[h]))
+
+            @pl.when(h == 0)
+            def _():
+                pass_w(heads - 1)
+
+        each_head(own_step)
 
     @pl.when(z >= 2)
     def _():
@@ -465,15 +484,17 @@
             def _():
                 pass_w(h + 2)
 
+            @pl.when(h > 0)
+            def _():
+                pass_att(h - 1)
+
         each_head(merge_step)
 
-    for other in others:
-
-        def pass_att(h, other=other):
-            att_wait(other, h)
-            att_pair(other, h, tok_half).start()
-
-        each_head(pass_att)
+    last = heads - 1
+
+    @pl.when(z < 2)
+    def _():
+        lax.fori_loop(0, last, lambda h, c: (pass_att(h), c)[1], 0)
 
     @pl.when(block_core(x) == s)
     def _():
@@ -483,36 +504,71 @@
     def _():
         each_head(lambda i: own_share(i).wait_recv())
 
-    def last_waits(h):
+    def pair_wait(h):
+        for other in others:
+            att_pair(other, h, sib_half).wait_recv()
+        att_pair(x, h, sib_half).wait_recv()
+
+    def early_waits(h):
         for other in others:
             for dy in range(1, n_str):
                 y_wait(other, dy, h)
-            att_pair(other, h, sib_half).wait_recv()
-        att_pair(x, h, sib_half).wait_recv()
-
-    each_head(last_waits)
+
+        @pl.when(h < last)
+        def _():
+            pair_wait(h)
+
+    each_head(early_waits)
 
     step = step_ref[z]
 
-    def gathered(rows):
-        return jnp.concatenate([att[i, rows] for i in range(n_head * heads)], axis=1)
-
-    attended = jnp.concatenate([gathered(sib_half), gathered(tok_half)], axis=0)
+    def gathered(h_from, h_to):
+        wanted = [src * heads + h for src in range(n_head) for h in range(h_from, h_to)]
+        return jnp.concatenate(
+            [
+                jnp.concatenate([att[i, rows] for i in wanted], axis=1)
+                for rows in (sib_half, tok_half)
+            ],
+            axis=0,
+        )
+
+    def weights(h_from, h_to, at):
+        return jnp.concatenate(
+            [w_full[(src * heads + h_from) * HD : (src * heads + h_to) * HD, at] for src in range(n_head)],
+            axis=0,
+        )
+
+    def tile_at(t):
+        return pl.ds(pl.multiple_of(t * tile, tile), tile)
+
+    attended = gathered(0, last)
 
     def project(t, carry):
-        at = pl.ds(pl.multiple_of(t * tile, tile), tile)
-        projected = jnp.dot(attended, w_full[:, at], preferred_element_type=jnp.float32)
+        projected[t] = jnp.dot(
+            attended, weights(0, last, tile_at(t)), preferred_element_type=jnp.float32
+        )
+        return carry
+
+    lax.fori_loop(0, tiles, project, 0)
+    pass_att(last)
+    pair_wait(last)
+    attended_last = gathered(last, heads)
+
+    def project_last(t, carry):
+        whole = projected[t] + jnp.dot(
+            attended_last, weights(last, heads, tile_at(t)), preferred_element_type=jnp.float32
+        )
         here = out_cols(s, t)
         gate_row = jnp.zeros((1, tile), jnp.float32)
         for i in range(gate_ref.shape[0]):
             gate_row = jnp.where(step == i, gate_ref[i : i + 1, here], gate_row)
-        gated = (gate_row * projected).astype(jnp.bfloat16)
+        gated = (gate_row * whole).astype(jnp.bfloat16)
         out_half[t] = gated[:tok]
         out_piece(s, t).start()
         out_ref[:, here] = gated[tok:]
         return carry
 
-    lax.fori_loop(0, tiles, project, 0)
+    lax.fori_loop(0, tiles, project_last, 0)
 
     def out_wait(t, carry):
         out_piece(sib, t).wait_recv()
@@ -608,6 +664,8 @@
                 vmem((n_head * heads * HD, half), low),
                 vmem((tiles, tok, tile), low),
                 vmem((n_head, heads, piece, half), low),
+                vmem((heads, HD, 2 * n_seq * tok), low),
+                vmem((tiles, n_seq * tok, tile), wide),
                 dma((n_head, heads)),
                 dma((n_head, heads)),
                 dma((3, heads)),

time: 48.2 us -> 48.2 us (level)
  no operation moved by 1% of the time
where the time goes in v5:
time: 48.2 us; the launch traced here: 48 us
  Pallas kernels  45.5 us (94%)
  local copies, waits for them, and re-layouts  2.46 us (5%)
    pallas_call x1, Pallas kernels, on_device(): pl.pallas_call(functools.partial(kernel, sizes), out_shape=jax.ShapeDtype...  45.5 us
    unnamed x1, local copies, waits for them, and re-layouts  2.46 us

profile of v5, /device:TPU:9, one launch (start us, length us, event | category | flops | bytes accessed | tf_op | source)
XLA Modules:
  0.0 48.0 jit_solution(12406713557418248054)
XLA Ops:
  0.0 45.5 %shard_map.73 = bf16[256,2560]{1,0:T(8,128)(2,1)} custom-call(s32[4]{0:T(128)} %step_ref.1, s32[4,4]{1,0:T(4,128)} %mask_ref.1, bf16[256,640]{1,0:T(8,128)(2,1)} %q_ref.1, bf16[256,640]{1,0:T(8,128)(2,1)} %k_ref.1, bf16[256,640]{1,0:T(8,128)(2,1)} %v_ref.1, bf16[640,2560]{1,0:T(8,128)(2,1)} %w_ref.1, f32[4,2560]{1,0:T(4,128)} %gate_ref.1), custom_call_target="tpu_custom_call" | custom-call | flops 3019898880 | bytes 9830400 | tf_op jit(solution)/shard_map/pallas_call | solution.py:638
  45.6 2.5 %copy.9 = bf16[256,2560]{1,0:T(8,128)(2,1)} copy(bf16[256,2560]{1,0:T(8,128)(2,1)} %shard_map.73) | data formatting | bytes 2621440

commit v6 on v5

--- a/solution.py
+++ b/solution.py
@@ -10,6 +10,7 @@
 
 HD = 128
 NEG_FLOOR = -1e30
+COPIES = 8
 MESH = pl.DeviceIdType.MESH
 SCORE_SCALE = math.log2(math.e) / math.sqrt(HD)
 
@@ -38,6 +39,8 @@
     att,
     w_full,
     out_half,
+    out_own,
+    out_store,
     w_relay,
     v_turned,
     projected,
@@ -84,7 +87,8 @@
     tile = 256 if half % 256 == 0 else 128
     tiles = half // tile
     y_rows = w_rows // n_str
-    piece = y_rows // heads
+    pieces = 2 * heads
+    piece = y_rows // pieces
     own_piece = w_rows // heads
 
     def remote(src, dst, ss, rs, **where):
@@ -97,6 +101,9 @@
 
     def each_head(body):
         lax.fori_loop(0, heads, lambda h, c: (body(h), c)[1], 0)
+
+    def each_piece(body):
+        lax.fori_loop(0, pieces, lambda i, c: (body(i), c)[1], 0)
 
     def down(body, low):
         lax.fori_loop(0, n_span - low, lambda i, c: (body(n_span - 1 - i), c)[1], 0)
@@ -254,6 +261,9 @@
             out_half.at[t], out_ref.at[:, out_cols(core, t)], out_send.at[t], out_recv.at[t], seq=sib
         )
 
+    def out_copy(t):
+        return pltpu.make_async_copy(out_own.at[t], out_ref.at[:, out_cols(s, t)], out_store.at[t])
+
     others = [lax.rem(x + dx, n_head) for dx in range(1, n_head)]
 
     barrier = pltpu.get_barrier_semaphore()
@@ -295,7 +305,7 @@
 
         @pl.when(block_core(other) == s)
         def _(other=other):
-            each_head(lambda i: (relay(other, i).start(), x_piece(other, i).start()))
+            each_piece(lambda i: (relay(other, i).start(), x_piece(other, i).start()))
 
     def block(q, keys, v_t, flags):
         scores = [
@@ -368,17 +378,18 @@
     def _():
         pass_on(0)
 
-    def pass_w(i):
-        for other in others:
-            x_wait(other, i)
-            for dy in range(1, n_str):
-                y_piece(other, dy, i).start()
+    def pass_w(h):
+        for i in (2 * h, 2 * h + 1):
+            for other in others:
+                x_wait(other, i)
+                for dy in range(1, n_str):
+                    y_piece(other, dy, i).start()
 
     for other in others:
 
         @pl.when(block_core(other) != s)
         def _(other=other):
-            each_head(lambda i: (relay(other, i).wait_recv(), x_relayed(other, i).start()))
+            each_piece(lambda i: (relay(other, i).wait_recv(), x_relayed(other, i).start()))
 
     def share_zero(h):
         zero_k(h).wait_recv()
@@ -440,13 +451,9 @@
         def _():
             emit(z, h, get_part(z, h))
 
-        @pl.when(z == 0)
+        @pl.when(z < 2)
         def _():
             pass_w(h)
-
-        @pl.when((z == 1) & (h > 0))
-        def _():
-            pass_w(h - 1)
 
         @pl.when((z >= 2) & ((h == 2) | (h == 4)))
         def _():
@@ -458,10 +465,6 @@
     def _():
         def own_step(h):
             emit(1, h, zero_block(1, h, v_turned[h]))
-
-            @pl.when(h == 0)
-            def _():
-                pass_w(heads - 1)
 
         each_head(own_step)
 
@@ -490,12 +493,6 @@
 
         each_head(merge_step)
 
-    last = heads - 1
-
-    @pl.when(z < 2)
-    def _():
-        lax.fori_loop(0, last, lambda h, c: (pass_att(h), c)[1], 0)
-
     @pl.when(block_core(x) == s)
     def _():
         each_head(lambda i: own_copy(i).wait())
@@ -504,60 +501,51 @@
     def _():
         each_head(lambda i: own_share(i).wait_recv())
 
-    def pair_wait(h):
-        for other in others:
-            att_pair(other, h, sib_half).wait_recv()
-        att_pair(x, h, sib_half).wait_recv()
-
-    def early_waits(h):
-        for other in others:
-            for dy in range(1, n_str):
-                y_wait(other, dy, h)
-
-        @pl.when(h < last)
-        def _():
-            pair_wait(h)
-
-    each_head(early_waits)
-
+    each_head(lambda h: att_pair(x, h, sib_half).wait_recv())
     step = step_ref[z]
 
-    def gathered(h_from, h_to):
-        wanted = [src * heads + h for src in range(n_head) for h in range(h_from, h_to)]
+    def gathered(src):
         return jnp.concatenate(
             [
-                jnp.concatenate([att[i, rows] for i in wanted], axis=1)
+                jnp.concatenate([att[src * heads + h, rows] for h in range(heads)], axis=1)
                 for rows in (sib_half, tok_half)
             ],
             axis=0,
         )
 
-    def weights(h_from, h_to, at):
-        return jnp.concatenate(
-            [w_full[(src * heads + h_from) * HD : (src * heads + h_to) * HD, at] for src in range(n_head)],
-            axis=0,
-        )
-
-    def tile_at(t):
-        return pl.ds(pl.multiple_of(t * tile, tile), tile)
-
-    attended = gathered(0, last)
+    def product(attended, src, t):
+        rows = pl.ds(pl.multiple_of(src * w_rows, w_rows), w_rows)
+        at = pl.ds(pl.multiple_of(t * tile, tile), tile)
+        return jnp.dot(attended, w_full[rows, at], preferred_element_type=jnp.float32)
+
+    attended_own = gathered(x)
 
     def project(t, carry):
-        projected[t] = jnp.dot(
-            attended, weights(0, last, tile_at(t)), preferred_element_type=jnp.float32
-        )
+        projected[t] = product(attended_own, x, t)
         return carry
 
     lax.fori_loop(0, tiles, project, 0)
-    pass_att(last)
-    pair_wait(last)
-    attended_last = gathered(last, heads)
+
+    @pl.when(z < 2)
+    def _():
+        lax.fori_loop(0, heads - 1, lambda h, c: (pass_att(h), c)[1], 0)
+
+    pass_att(heads - 1)
+
+    def other_waits(h):
+        for other in others:
+            for half_piece in range(2):
+                for dy in range(1, n_str):
+                    y_wait(other, dy, 2 * h + half_piece)
+            att_pair(other, h, sib_half).wait_recv()
+
+    each_head(other_waits)
+    attended_others = [gathered(other) for other in others]
 
     def project_last(t, carry):
-        whole = projected[t] + jnp.dot(
-            attended_last, weights(last, heads, tile_at(t)), preferred_element_type=jnp.float32
-        )
+        whole = projected[t]
+        for other, attended in zip(others, attended_others):
+            whole = whole + product(attended, other, t)
         here = out_cols(s, t)
         gate_row = jnp.zeros((1, tile), jnp.float32)
         for i in range(gate_ref.shape[0]):
@@ -565,7 +553,8 @@
         gated = (gate_row * whole).astype(jnp.bfloat16)
         out_half[t] = gated[:tok]
         out_piece(s, t).start()
-        out_ref[:, here] = gated[tok:]
+        out_own[t] = gated[tok:]
+        out_copy(t).start()
         return carry
 
     lax.fori_loop(0, tiles, project_last, 0)
@@ -573,6 +562,7 @@
     def out_wait(t, carry):
         out_piece(sib, t).wait_recv()
         out_piece(s, t).wait_send()
+        out_copy(t).wait()
         return carry
 
     lax.fori_loop(0, tiles, out_wait, 0)
@@ -583,39 +573,56 @@
         att_pair(x, h, tok_half).wait_send()
         for other in others:
             att_piece(other, h).wait_send()
+            att_pair(other, h, tok_half).wait_send()
+
+        @pl.when(block_core(x) == s)
+        def _():
+            own_share(h).wait_send()
+
+        @pl.when(z == 0)
+        def _():
+            zero_k(h).wait_send()
+            zero_v(h).wait_send()
+
+        @pl.when(z == 1)
+        def _():
+            fwd_k(h, tok_half).wait_send()
+            fwd_v(h, tok_half).wait_send()
+
+        @pl.when(z >= 2)
+        def _():
+            down(lambda c: pass_q(c, h).wait_send(), z)
+
+        @pl.when(z >= 1)
+        def _():
+            down(lambda c: (pass_acc(c, h).wait_send(), pass_stat(c, h).wait_send()), z + 1)
+
+    def sent_weights(i):
+        for other in others:
             for dy in range(1, n_str):
-                y_piece(other, dy, h).wait_send()
-            att_pair(other, h, tok_half).wait_send()
-
-            x_piece(other, h).wait_send()
+                y_piece(other, dy, i).wait_send()
+            x_piece(other, i).wait_send()
 
             @pl.when(block_core(other) == s)
             def _(other=other):
-                relay(other, h).wait_send()
-
-        @pl.when(block_core(x) == s)
-        def _():
-            own_share(h).wait_send()
-
-        @pl.when(z == 0)
-        def _():
-            zero_k(h).wait_send()
-            zero_v(h).wait_send()
-
-        @pl.when(z == 1)
-        def _():
-            fwd_k(h, tok_half).wait_send()
-            fwd_v(h, tok_half).wait_send()
-
-        @pl.when(z >= 2)
-        def _():
-            down(lambda c: pass_q(c, h).wait_send(), z)
-
-        @pl.when(z >= 1)
-        def _():
-            down(lambda c: (pass_acc(c, h).wait_send(), pass_stat(c, h).wait_send()), z + 1)
+                relay(other, i).wait_send()
 
     each_head(sent)
+    each_piece(sent_weights)
+
+
+def hand_over(from_ref, to_ref, sems):
+    rows = from_ref.shape[0] // COPIES
+    copies = [
+        pltpu.make_async_copy(
+            from_ref.at[i * rows : (i + 1) * rows], to_ref.at[i * rows : (i + 1) * rows], sems.at[i]
+        )
+        for i in range(COPIES)
+    ]
+    for copy in copies:
+        copy.start()
+    for copy in copies:
+        copy.wait()
 
 
 def solution(mesh):
@@ -630,12 +637,13 @@
         half = cols // n_seq
         tile = 256 if half % 256 == 0 else 128
         tiles = half // tile
-        piece = out_weight.shape[0] // n_str // heads
+        pieces = 2 * heads
+        piece = out_weight.shape[0] // n_str // pieces
         vmem, any_space = pltpu.VMEM, pl.ANY
         dma = pltpu.SemaphoreType.DMA
         low, wide = jnp.bfloat16, jnp.float32
         flops = 4 * heads * tok * tok * n_seq * n_span * HD + 2 * tok * n_head * heads * HD * cols
-        return pl.pallas_call(
+        result = pl.pallas_call(
             functools.partial(kernel, sizes),
             out_shape=jax.ShapeDtypeStruct((tok, cols), low),
             in_specs=[
@@ -647,7 +655,7 @@
                 pl.BlockSpec(memory_space=any_space),
                 pl.BlockSpec(memory_space=vmem),
             ],
-            out_specs=pl.BlockSpec(memory_space=vmem),
+            out_specs=pl.BlockSpec(memory_space=any_space),
             scratch_shapes=[
                 vmem((n_span, heads, tok, HD), low),
                 vmem((heads, n_seq * tok, HD), low),
@@ -663,11 +671,13 @@
                 vmem((n_head * heads, n_seq * tok, HD), low),
                 vmem((n_head * heads * HD, half), low),
                 vmem((tiles, tok, tile), low),
-                vmem((n_head, heads, piece, half), low),
+                vmem((tiles, tok, tile), low),
+                dma((tiles,)),
+                vmem((n_head, pieces, piece, half), low),
                 vmem((heads, HD, 2 * n_seq * tok), low),
                 vmem((tiles, n_seq * tok, tile), wide),
-                dma((n_head, heads)),
-                dma((n_head, heads)),
+                dma((n_head, pieces)),
+                dma((n_head, pieces)),
                 dma((3, heads)),
                 dma((2, heads)),
                 dma((2, heads)),
@@ -681,10 +691,10 @@
                 dma((n_span, heads)),
                 dma((n_span, heads)),
                 dma((n_span, heads)),
-                dma((n_head, heads)),
-                dma((n_head, heads)),
-                dma((n_head, n_str, heads)),
-                dma((n_head, n_str, heads)),
+                dma((n_head, pieces)),
+                dma((n_head, pieces)),
+                dma((n_head, n_str, pieces)),
+                dma((n_head, n_str, pieces)),
                 dma((heads,)),
                 dma((heads,)),
                 dma((heads,)),
@@ -702,6 +712,13 @@
                 flops=flops, bytes_accessed=6 * out_weight.size, transcendentals=0
             ),
         )(step_index, block_mask, query_rows, key_rows, value_rows, out_weight, gate_table)
+        return pl.pallas_call(
+            hand_over,
+            out_shape=jax.ShapeDtypeStruct((tok, cols), low),
+            in_specs=[pl.BlockSpec(memory_space=any_space)],
+            out_specs=pl.BlockSpec(memory_space=any_space),
+            scratch_shapes=[dma((COPIES,))],
+        )(result)
 
     in_specs = (
         P(("streams", "span", "seq"), "head"),

time: 48.2 us -> 84.3 us (1.75)
  the two profiles are of different devices: /device:TPU:9 before, /device:TPU:29 now
where the time goes in v6:
time: 84.3 us; the launch traced here: 84.1 us
  Pallas kernels  84.1 us (100%)
    pallas_call x1, Pallas kernels, on_device(): pl.pallas_call(functools.partial(kernel, sizes), out_shape=jax.ShapeDtype...  43.2 us
    pallas_call x1, Pallas kernels, on_device(): pl.pallas_call(hand_over, out_shape=jax.ShapeDtypeStruct((tok, cols), low...  40.9 us

profile of v6, /device:TPU:29, one launch (start us, length us, event | category | flops | bytes accessed | tf_op | source)
XLA Modules:
  0.0 84.1 jit_solution(17594522242176750297)
XLA Ops:
  0.0 43.2 %shard_map.73.from_ref = bf16[256,2560]{1,0:T(8,128)(2,1)} custom-call(s32[4]{0:T(128)} %step_ref.1, s32[4,4]{1,0:T(4,128)} %mask_ref.1, bf16[256,640]{1,0:T(8,128)(2,1)} %q_ref.1, bf16[256,640]{1,0:T(8,128)(2,1)} %k_ref.1, bf16[256,640]{1,0:T(8,128)(2,1)} %v_ref.1, bf16[640,2560]{1,0:T(8,128)(2,1)} %w_ref.1, f32[4,2560]{1,0:T(4,128)} %gate_ref.1), custom_call_target="tpu_custom_call" | custom-call | flops 3019898880 | bytes 9830400 | tf_op jit(solution)/shard_map/pallas_call | solution.py:646
  43.2 40.9 %shard_map.74 = bf16[256,2560]{1,0:T(8,128)(2,1)} custom-call(bf16[256,2560]{1,0:T(8,128)(2,1)} %shard_map.73.from_ref), custom_call_target="tpu_custom_call" | custom-call | tf_op jit(solution)/shard_map/pallas_call | solution.py:715

commit v7 on v6

--- a/solution.py
+++ b/solution.py
@@ -10,7 +10,7 @@
 
 HD = 128
 NEG_FLOOR = -1e30
-COPIES = 8
+COPIES = 4
 MESH = pl.DeviceIdType.MESH
 SCORE_SCALE = math.log2(math.e) / math.sqrt(HD)
 
@@ -42,6 +42,10 @@
     out_own,
     out_store,
     w_relay,
+    w_stage,
+    own_stage,
+    stage_sem,
+    share_sem,
     v_turned,
     projected,
     relay_send,
@@ -178,10 +182,22 @@
         first = lax.rem(dst_x, n_head // n_seq) * cols + core * half
         return pl.ds(pl.multiple_of(first, HD), half)
 
+    def piece_rows(i):
+        return pl.ds(pl.multiple_of(i * piece, piece), piece)
+
+    def load_w(dst_x, core):
+        return pltpu.make_async_copy(
+            w_ref.at[pl.ds(pl.multiple_of(y * y_rows, y_rows), y_rows), block_cols(dst_x, core)],
+            w_stage.at[dst_x, core],
+            stage_sem.at[dst_x, core],
+        )
+
+    def load_share():
+        return pltpu.make_async_copy(w_ref.at[:, block_cols(x, sib)], own_stage, share_sem.at[0])
+
     def x_piece(dst_x, i):
-        first = y * y_rows + i * piece
-        return remote(
-            w_ref.at[pl.ds(pl.multiple_of(first, piece), piece), block_cols(dst_x, s)],
+        return remote(
+            w_stage.at[dst_x, s, piece_rows(i)],
             w_at(x, y, i),
             x_send.at[dst_x, i],
             x_recv.at[x, i],
@@ -189,9 +205,8 @@
         )
 
     def relay(dst_x, i):
-        first = y * y_rows + i * piece
-        return remote(
-            w_ref.at[pl.ds(pl.multiple_of(first, piece), piece), block_cols(dst_x, sib)],
+        return remote(
+            w_stage.at[dst_x, sib, piece_rows(i)],
             w_relay.at[dst_x, i],
             relay_send.at[dst_x, i],
             relay_recv.at[dst_x, i],
@@ -238,7 +253,7 @@
 
     def own_share(i):
         return remote(
-            w_ref.at[own_rows(i), block_cols(x, sib)], own_at(i), own_send.at[i], own_recv.at[i], seq=sib
+            own_stage.at[own_rows(i)], own_at(i), own_send.at[i], own_recv.at[i], seq=sib
         )
 
     def att_piece(dst_x, h):
@@ -287,6 +302,17 @@
         greet(span=z + 1)
 
     each_head(lambda h: (load_q(h).start(), load_k(h).start(), load_v(h).start()))
+    for other in others:
+
+        @pl.when(block_core(other) == s)
+        def _(other=other):
+            for core in range(n_seq):
+                load_w(other, core).start()
+
+    @pl.when(block_core(x) == s)
+    def _():
+        load_share().start()
+
     beside = jnp.where(z > 0, 1, 0) + jnp.where(z < n_span - 1, 1, 0)
     pl.semaphore_wait(barrier, 1 + n_seq * (n_head - 1) + (n_str - 1) + beside)
 
@@ -305,7 +331,13 @@
 
         @pl.when(block_core(other) == s)
         def _(other=other):
+            for core in range(n_seq):
+                load_w(other, core).wait()
             each_piece(lambda i: (relay(other, i).start(), x_piece(other, i).start()))
+
+    @pl.when(block_core(x) == s)
+    def _():
+        load_share().wait()
 
     def block(q, keys, v_t, flags):
         scores = [
@@ -611,18 +643,8 @@
     each_piece(sent_weights)
 
 
-def hand_over(from_ref, to_ref, sems):
-    rows = from_ref.shape[0] // COPIES
-    copies = [
-        pltpu.make_async_copy(
-            from_ref.at[i * rows : (i + 1) * rows], to_ref.at[i * rows : (i + 1) * rows], sems.at[i]
-        )
-        for i in range(COPIES)
-    ]
-    for copy in copies:
-        copy.start()
-    for copy in copies:
-        copy.wait()
+def hand_over(from_ref, to_ref):
+    to_ref[...] = from_ref[...]
 
 
 def solution(mesh):
@@ -674,6 +696,10 @@
                 vmem((tiles, tok, tile), low),
                 dma((tiles,)),
                 vmem((n_head, pieces, piece, half), low),
+                vmem((n_head, n_seq, pieces * piece, half), low),
+                vmem((out_weight.shape[0], half), low),
+                dma((n_head, n_seq)),
+                dma((1,)),
                 vmem((heads, HD, 2 * n_seq * tok), low),
                 vmem((tiles, n_seq * tok, tile), wide),
                 dma((n_head, pieces)),
@@ -712,12 +738,13 @@
                 flops=flops, bytes_accessed=6 * out_weight.size, transcendentals=0
             ),
         )(step_index, block_mask, query_rows, key_rows, value_rows, out_weight, gate_table)
+        rows = pl.BlockSpec((tok // COPIES, cols), lambda i: (i, 0))
         return pl.pallas_call(
             hand_over,
             out_shape=jax.ShapeDtypeStruct((tok, cols), low),
-            in_specs=[pl.BlockSpec(memory_space=any_space)],
-            out_specs=pl.BlockSpec(memory_space=any_space),
-            scratch_shapes=[dma((COPIES,))],
+            grid=(COPIES,),
+            in_specs=[rows],
+            out_specs=rows,
         )(result)
 
     in_specs = (

time: 84.3 us -> 46.7 us (0.55)
  Pallas kernels: 84.1 us -> 46.5 us
    pallas_call x1, Pallas kernels: 40.9 us -> 3.47 us  [on_device(): pl.pallas_call(hand_over, out_shape=jax.ShapeDtypeStruct((tok, cols), low...]
where the time goes in v7:
time: 46.7 us; the launch traced here: 46.5 us
  Pallas kernels  46.5 us (100%)
    pallas_call x1, Pallas kernels, on_device(): pl.pallas_call(functools.partial(kernel, sizes), out_shape=jax.ShapeDtype...  43 us
    pallas_call x1, Pallas kernels, on_device(): pl.pallas_call(hand_over, out_shape=jax.ShapeDtypeStruct((tok, cols), low...  3.47 us

profile of v7, /device:TPU:29, one launch (start us, length us, event | category | flops | bytes accessed | tf_op | source)
XLA Modules:
  0.0 46.5 jit_solution(2082007304316139519)
XLA Ops:
  0.0 43.0 %shard_map.73.from_ref = bf16[256,2560]{1,0:T(8,128)(2,1)} custom-call(s32[4]{0:T(128)} %step_ref.1, s32[4,4]{1,0:T(4,128)} %mask_ref.1, bf16[256,640]{1,0:T(8,128)(2,1)} %q_ref.1, bf16[256,640]{1,0:T(8,128)(2,1)} %k_ref.1, bf16[256,640]{1,0:T(8,128)(2,1)} %v_ref.1, bf16[640,2560]{1,0:T(8,128)(2,1)} %w_ref.1, f32[4,2560]{1,0:T(4,128)} %gate_ref.1), custom_call_target="tpu_custom_call" | custom-call | flops 3019898880 | bytes 9830400 | tf_op jit(solution)/shard_map/pallas_call | solution.py:668
  43.0 3.5 %shard_map.74 = bf16[256,2560]{1,0:T(8,128)(2,1)} custom-call(bf16[256,2560]{1,0:T(8,128)(2,1)} %shard_map.73.from_ref), custom_call_target="tpu_custom_call" | custom-call | tf_op jit(solution)/shard_map/pallas_call | solution.py:742

commit v8 on v7

--- a/solution.py
+++ b/solution.py
@@ -10,7 +10,6 @@
 
 HD = 128
 NEG_FLOOR = -1e30
-COPIES = 4
 MESH = pl.DeviceIdType.MESH
 SCORE_SCALE = math.log2(math.e) / math.sqrt(HD)
 
@@ -163,13 +162,19 @@
 
     def pass_acc(c, h):
         return remote(
-            acc_out.at[c, h], acc_in.at[c, h], acc_send.at[c, h], acc_recv.at[c, h], span=z + 1
+            acc_out.at[c, h], acc_in.at[z, h], acc_send.at[c, h], acc_recv.at[z, h], span=c
         )
 
     def pass_stat(c, h):
         return remote(
-            stat_out.at[c, h], stat_in.at[c, h], stat_send.at[c, h], stat_recv.at[c, h], span=z + 1
-        )
+            stat_out.at[c, h], stat_in.at[z, h], stat_send.at[c, h], stat_recv.at[z, h], span=c
+        )
+
+    def take_part(e, h):
+        acc, stat = acc_in.at[e, h], stat_in.at[e, h]
+        remote(acc, acc, acc_send.at[e, h], acc_recv.at[e, h], span=e).wait_recv()
+        remote(stat, stat, stat_send.at[e, h], stat_recv.at[e, h], span=e).wait_recv()
+        return stat_in[e, h, 0:1], stat_in[e, h, 1:2], acc_in[e, h].astype(jnp.float32)
 
     def w_at(src_x, part, i):
         first = src_x * w_rows + part * y_rows + i * piece
@@ -293,13 +298,8 @@
     for dy in range(1, n_str):
         greet(streams=lax.rem(y + dy, n_str))
 
-    @pl.when(z > 0)
-    def _():
-        greet(span=z - 1)
-
-    @pl.when(z < n_span - 1)
-    def _():
-        greet(span=z + 1)
+    for dz in range(1, n_span):
+        greet(span=lax.rem(z + dz, n_span))
 
     each_head(lambda h: (load_q(h).start(), load_k(h).start(), load_v(h).start()))
     for other in others:
@@ -313,8 +313,7 @@
     def _():
         load_share().start()
 
-    beside = jnp.where(z > 0, 1, 0) + jnp.where(z < n_span - 1, 1, 0)
-    pl.semaphore_wait(barrier, 1 + n_seq * (n_head - 1) + (n_str - 1) + beside)
+    pl.semaphore_wait(barrier, 1 + n_seq * (n_head - 1) + (n_str - 1) + (n_span - 1))
 
     each_head(lambda h: (load_q(h).wait(), load_k(h).wait(), load_v(h).wait()))
 
@@ -363,29 +362,26 @@
         wa, wb = jnp.exp2(a[0] - top), jnp.exp2(b[0] - top)
         return top, wa * a[1] + wb * b[1], wa * a[2] + wb * b[2]
 
-    def get_part(c, h):
-        return part_stat[c, h, 0:1], part_stat[c, h, 1:2], part_acc[c, h]
-
-    def put_part(c, h, part):
-        part_stat[c, h, 0:1] = part[0]
-        part_stat[c, h, 1:2] = part[1]
-        part_acc[c, h] = part[2]
-
-    def emit(c, h, part):
-        @pl.when(c > z)
-        def _():
-            stat_out[c, h, 0:1] = part[0]
-            stat_out[c, h, 1:2] = part[1]
-            acc_out[c, h] = part[2].astype(jnp.bfloat16)
-            pass_acc(c, h).start()
-            pass_stat(c, h).start()
-
-        @pl.when(c == z)
-        def _():
-            att[x * heads + h, tok_half] = (part[2] / part[1]).T.astype(jnp.bfloat16)
-            for other in others:
-                att_piece(other, h).start()
-            att_pair(x, h, tok_half).start()
+    def get_part(h):
+        return part_stat[h, 0:1], part_stat[h, 1:2], part_acc[h]
+
+    def put_part(h, part):
+        part_stat[h, 0:1] = part[0]
+        part_stat[h, 1:2] = part[1]
+        part_acc[h] = part[2]
+
+    def send_part(c, h, part):
+        stat_out[c, h, 0:1] = part[0]
+        stat_out[c, h, 1:2] = part[1]
+        acc_out[c, h] = part[2].astype(jnp.bfloat16)
+        pass_acc(c, h).start()
+        pass_stat(c, h).start()
+
+    def finish(h, part):
+        att[x * heads + h, tok_half] = (part[2] / part[1]).T.astype(jnp.bfloat16)
+        for other in others:
+            att_piece(other, h).start()
+        att_pair(x, h, tok_half).start()
 
     def pass_att(h):
         for other in others:
@@ -459,9 +455,18 @@
         @pl.when(z != 1)
         def _():
             def own_block(c):
-                put_part(c, h, block(q_all[c, h], [k_here], v_here, [mask_ref[c, z]]))
-
-            down(own_block, z)
+                part = block(q_all[c, h], [k_here], v_here, [mask_ref[c, z]])
+
+                @pl.when(c > z)
+                def _():
+                    send_part(c, h, part)
+
+                @pl.when(c == z)
+                def _():
+                    put_part(h, part)
+
+            served = jnp.where(z == 0, 1, n_span - z)
+            lax.fori_loop(0, served, lambda i, c: (own_block(z + served - 1 - i), c)[1], 0)
 
         @pl.when(z == 1)
         def _():
@@ -471,7 +476,7 @@
             v_turned[h] = both
 
             def later(c):
-                emit(c, h, zero_block(c, h, both))
+                send_part(c, h, zero_block(c, h, both))
 
                 @pl.when((c == n_span - 1) & (h + 1 < heads))
                 def _():
@@ -481,7 +486,7 @@
 
         @pl.when(z == 0)
         def _():
-            emit(z, h, get_part(z, h))
+            finish(h, get_part(h))
 
         @pl.when(z < 2)
         def _():
@@ -496,24 +501,19 @@
     @pl.when(z == 1)
     def _():
         def own_step(h):
-            emit(1, h, zero_block(1, h, v_turned[h]))
+            finish(h, zero_block(1, h, v_turned[h]))
 
         each_head(own_step)
 
     @pl.when(z >= 2)
     def _():
         def merge_step(h):
-            def one(c):
-                pass_acc(c, h).wait_recv()
-                pass_stat(c, h).wait_recv()
-                before = (
-                    stat_in[c, h, 0:1],
-                    stat_in[c, h, 1:2],
-                    acc_in[c, h].astype(jnp.float32),
-                )
-                emit(c, h, merge(get_part(c, h), before))
-
-            down(one, z)
+            def one(i, carry):
+                put_part(h, merge(get_part(h), take_part(z - 1 - i, h)))
+                return carry
+
+            lax.fori_loop(0, z - 1, one, 0)
+            finish(h, get_part(h))
 
             @pl.when(h + 2 < heads)
             def _():
@@ -643,10 +643,6 @@
     each_piece(sent_weights)
 
 
-def hand_over(from_ref, to_ref):
-    to_ref[...] = from_ref[...]
-
-
 def solution(mesh):
     n_str, n_span = mesh.shape["streams"], mesh.shape["span"]
     n_head, n_seq = mesh.shape["head"], mesh.shape["seq"]
@@ -665,7 +661,7 @@
         dma = pltpu.SemaphoreType.DMA
         low, wide = jnp.bfloat16, jnp.float32
         flops = 4 * heads * tok * tok * n_seq * n_span * HD + 2 * tok * n_head * heads * HD * cols
-        result = pl.pallas_call(
+        return pl.pallas_call(
             functools.partial(kernel, sizes),
             out_shape=jax.ShapeDtypeStruct((tok, cols), low),
             in_specs=[
@@ -684,8 +680,8 @@
                 vmem((heads, n_seq * tok, HD), low),
                 vmem((heads, n_seq * tok, HD), low),
                 vmem((heads, n_seq * tok, HD), low),
-                vmem((n_span, heads, HD, tok), wide),
-                vmem((n_span, heads, 8, tok), wide),
+                vmem((heads, HD, tok), wide),
+                vmem((heads, 8, tok), wide),
                 vmem((n_span, heads, HD, tok), low),
                 vmem((n_span, heads, 8, tok), wide),
                 vmem((n_span, heads, HD, tok), low),
@@ -738,14 +734,6 @@
                 flops=flops, bytes_accessed=6 * out_weight.size, transcendentals=0
             ),
         )(step_index, block_mask, query_rows, key_rows, value_rows, out_weight, gate_table)
-        rows = pl.BlockSpec((tok // COPIES, cols), lambda i: (i, 0))
-        return pl.pallas_call(
-            hand_over,
-            out_shape=jax.ShapeDtypeStruct((tok, cols), low),
-            grid=(COPIES,),
-            in_specs=[rows],
-            out_specs=rows,
-        )(result)
 
     in_specs = (
         P(("streams", "span", "seq"), "head"),

time: 46.7 us -> 44.5 us (0.953)
  the two profiles are of different devices: /device:TPU:29 before, /device:TPU:9 now
where the time goes in v8:
time: 44.5 us; the launch traced here: 44.1 us
  Pallas kernels  41.6 us (93%)
  local copies, waits for them, and re-layouts  2.46 us (6%)
    pallas_call x1, Pallas kernels, on_device(): pl.pallas_call(functools.partial(kernel, sizes), out_shape=jax.ShapeDtype...  41.6 us
    unnamed x1, local copies, waits for them, and re-layouts  2.46 us

profile of v8, /device:TPU:9, one launch (start us, length us, event | category | flops | bytes accessed | tf_op | source)
XLA Modules:
  0.0 44.1 jit_solution(3634824395519500998)
XLA Ops:
  0.0 41.6 %shard_map.73 = bf16[256,2560]{1,0:T(8,128)(2,1)} custom-call(s32[4]{0:T(128)} %step_ref.1, s32[4,4]{1,0:T(4,128)} %mask_ref.1, bf16[256,640]{1,0:T(8,128)(2,1)} %q_ref.1, bf16[256,640]{1,0:T(8,128)(2,1)} %k_ref.1, bf16[256,640]{1,0:T(8,128)(2,1)} %v_ref.1, bf16[640,2560]{1,0:T(8,128)(2,1)} %w_ref.1, f32[4,2560]{1,0:T(4,128)} %gate_ref.1), custom_call_target="tpu_custom_call" | custom-call | flops 3019898880 | bytes 9830400 | tf_op jit(solution)/shard_map/pallas_call | solution.py:664
  41.6 2.5 %copy.9 = bf16[256,2560]{1,0:T(8,128)(2,1)} copy(bf16[256,2560]{1,0:T(8,128)(2,1)} %shard_map.73) | data formatting | bytes 2621440

commit v9 on v8

--- a/solution.py
+++ b/solution.py
@@ -301,7 +301,6 @@
     for dz in range(1, n_span):
         greet(span=lax.rem(z + dz, n_span))
 
-    each_head(lambda h: (load_q(h).start(), load_k(h).start(), load_v(h).start()))
     for other in others:
 
         @pl.when(block_core(other) == s)
@@ -309,23 +308,14 @@
             for core in range(n_seq):
                 load_w(other, core).start()
 
+    each_head(lambda h: (load_q(h).start(), load_k(h).start(), load_v(h).start()))
+
     @pl.when(block_core(x) == s)
     def _():
         load_share().start()
 
     pl.semaphore_wait(barrier, 1 + n_seq * (n_head - 1) + (n_str - 1) + (n_span - 1))
 
-    each_head(lambda h: (load_q(h).wait(), load_k(h).wait(), load_v(h).wait()))
-
-    @pl.when(z >= 2)
-    def _():
-        pass_q(z, 0).start()
-
-    @pl.when(z == 0)
-    def _():
-        each_head(lambda h: (zero_k(h).start(), zero_v(h).start()))
-
-    each_head(lambda h: (sib_k(h, tok_half).start(), sib_v(h, tok_half).start()))
     for other in others:
 
         @pl.when(block_core(other) == s)
@@ -333,6 +323,23 @@
             for core in range(n_seq):
                 load_w(other, core).wait()
             each_piece(lambda i: (relay(other, i).start(), x_piece(other, i).start()))
+
+    each_head(lambda h: (load_q(h).wait(), load_k(h).wait(), load_v(h).wait()))
+
+    @pl.when(z >= 2)
+    def _():
+        pass_q(z, 0).start()
+
+    @pl.when(z == 0)
+    def _():
+        each_head(lambda h: (zero_k(h).start(), zero_v(h).start()))
+
+    each_head(lambda h: (sib_k(h, tok_half).start(), sib_v(h, tok_half).start()))
+    for other in others:
+
+        @pl.when(block_core(other) != s)
+        def _(other=other):
+            each_piece(lambda i: (relay(other, i).wait_recv(), x_relayed(other, i).start()))
 
     @pl.when(block_core(x) == s)
     def _():
@@ -412,12 +419,6 @@
                 x_wait(other, i)
                 for dy in range(1, n_str):
                     y_piece(other, dy, i).start()
-
-    for other in others:
-
-        @pl.when(block_core(other) != s)
-        def _(other=other):
-            each_piece(lambda i: (relay(other, i).wait_recv(), x_relayed(other, i).start()))
 
     def share_zero(h):
         zero_k(h).wait_recv()

time: 44.5 us -> 44.8 us (level)
  no operation moved by 1% of the time
where the time goes in v9:
time: 44.8 us; the launch traced here: 44.2 us
  Pallas kernels  41.7 us (93%)
  local copies, waits for them, and re-layouts  2.46 us (5%)
    pallas_call x1, Pallas kernels, on_device(): pl.pallas_call(functools.partial(kernel, sizes), out_shape=jax.ShapeDtype...  41.7 us
    unnamed x1, local copies, waits for them, and re-layouts  2.46 us

profile of v9, /device:TPU:9, one launch (start us, length us, event | category | flops | bytes accessed | tf_op | source)
XLA Modules:
  0.0 44.2 jit_solution(12784285215842396960)
XLA Ops:
  0.0 41.7 %shard_map.73 = bf16[256,2560]{1,0:T(8,128)(2,1)} custom-call(s32[4]{0:T(128)} %step_ref.1, s32[4,4]{1,0:T(4,128)} %mask_ref.1, bf16[256,640]{1,0:T(8,128)(2,1)} %q_ref.1, bf16[256,640]{1,0:T(8,128)(2,1)} %k_ref.1, bf16[256,640]{1,0:T(8,128)(2,1)} %v_ref.1, bf16[640,2560]{1,0:T(8,128)(2,1)} %w_ref.1, f32[4,2560]{1,0:T(4,128)} %gate_ref.1), custom_call_target="tpu_custom_call" | custom-call | flops 3019898880 | bytes 9830400 | tf_op jit(solution)/shard_map/pallas_call | solution.py:665
  41.7 2.5 %copy.9 = bf16[256,2560]{1,0:T(8,128)(2,1)} copy(bf16[256,2560]{1,0:T(8,128)(2,1)} %shard_map.73) | data formatting | bytes 2621440
